TPU v7x, 128 devices: a whole 4x4x4 slice. The times are simulated.
128 devices in a mesh: grp: 2 (over core), row: 16 (over y, x), col: 4 (over z).
Axes of the slice: x: 4, y: 4, z: 4, core: 2. Of those that a mesh axis runs over, the one named last changes fastest.
Arguments:
- channels: bfloat16 [6, 4096, 8192], P('grp', 'row', 'col'), may hold values from -0.06629126 to 0.06629126, as said below
- inverse: float32 [6, 4096, 4096], P('grp', 'row', 'col'), may hold values from -1 to 1, as said below
- arrivals: bfloat16 [6, 3, 192, 8192], P(None, None, ('grp', 'row'), 'col'), may hold values from -0.06629126 to 0.06629126
- arrival_cell: int32 [6, 3, 128, 1], replicated, may hold values from 0 to 31; in each aligned block of 128 rows (0 to 127, 128 to 255, ..., all dimensions but the last counted through in order) at most 6 rows name the same one
- cell_owner: int32 [32], replicated, may hold values from 0 to 31, each once
- slots: int32 [6, 3, 128], replicated, may hold values from 0 to 4095, as said below
- symbols: bfloat16 [6, 4096, 256], P('grp', 'col'), may hold values from -45 to 45
Outputs:
- updated_inverse: float32 [6, 4096, 4096], P('grp', 'row', 'col')
- transmit: float32 [256, 6, 8192], P('row', 'grp', 'col')
Inputs may be any that keep to these rules, and one draw needn't show every extreme that they name: In each group the 3 x 128 slots are distinct. `inverse`: Symmetric; in each group the rows and columns at that group's slots are those of the identity. `channels`: rows at a group's slots are zero. `arrival_cell`: in each group and epoch at most 6 arriving users share a cell.
All inputs are finite; a program needn't handle non-finite values.
Results may differ from a plain program's by a relative error of at most 0.0031.
Values may be sent and summed in bfloat16 or wider, within the bound.
No kernel may reach another device: no remote copies, remote signals or barrier semaphores. Data moves between devices by JAX's collectives and lax.ppermute only.
A program may use at most 128 MiB of HBM per device.

v0:
```python
import jax
import jax.numpy as jnp
from jax import lax
from jax.experimental import pallas as pl
from jax.experimental.pallas import tpu as pltpu
from jax.sharding import PartitionSpec as P

ANTENNAS = 8192
ARRIVE = 128
EPOCHS = 3
STREAMS = 256
TOTAL = ARRIVE * EPOCHS
BLOCK = 128
PANEL = 8
WINDOW = 48
SHARE = TOTAL // 16
SHARE_PAD = 32

loading = 1.0
epsilon = 1e-06
highest = lax.Precision.HIGHEST
f32 = jnp.float32
bf16 = jnp.bfloat16
VMEM = pl.BlockSpec(memory_space=pltpu.VMEM)
SMEM = pl.BlockSpec(memory_space=pltpu.SMEM)
ANY = pl.BlockSpec(memory_space=pl.ANY)


def params():
    return pltpu.CompilerParams(vmem_limit_bytes=40 * 1024 * 1024)


def cost(flops, nbytes):
    return pl.CostEstimate(flops=flops, bytes_accessed=nbytes, transcendentals=0)


def dot(a, b):
    return jnp.dot(a, b, preferred_element_type=f32)


def dot_t(a, b):
    return lax.dot_general(a, b, (((1,), (1,)), ((), ())), preferred_element_type=f32)


def t_dot(a, b):
    return lax.dot_general(a, b, (((0,), (0,)), ((), ())), preferred_element_type=f32)


def halves(a):
    high = a.astype(bf16)
    return high, (a - high.astype(f32)).astype(bf16)


def split(product, a, b):
    a_high, a_low = halves(a)
    b_high, b_low = halves(b)
    return product(a_high, b_low) + product(a_low, b_high) + product(a_high, b_high)


def placing(slots_ref, first, rows):
    ids = first + lax.broadcasted_iota(jnp.int32, (rows, TOTAL), 0)
    return (ids == slots_ref[...].reshape(1, TOTAL)).astype(f32)


def choosing(place_ref, g):
    ids = lax.broadcasted_iota(jnp.int32, (16 * WINDOW, TOTAL), 0)
    return (ids == place_ref[g]).astype(f32).astype(bf16)


def start_windows(gathered_ref, window_ref, sems, groups, per_group):
    copies = []
    for g in range(groups):
        start = g * per_group // 16 * 16
        copy = pltpu.make_async_copy(
            gathered_ref.at[:, pl.ds(start, WINDOW), :], window_ref.at[g], sems.at[g]
        )
        copy.start()
        copies.append(copy)
    return copies


def columns_kernel(gathered_ref, channel_ref, place_ref, few_ref, out_ref, window_ref, sems):
    groups, user_rows, antennas = channel_ref.shape
    copies = start_windows(gathered_ref, window_ref, sems, groups, 2 * EPOCHS * 6)
    out_ref[groups] = jnp.zeros(out_ref.shape[1:], bf16)
    for g in range(groups):
        choose = choosing(place_ref, g)
        lanes = lax.broadcasted_iota(jnp.int32, (SHARE_PAD, 16 * WINDOW), 1)
        choose_few = (lanes == few_ref[g]).astype(f32).astype(bf16)
        copies[g].wait()
        window = window_ref[g].reshape(16 * WINDOW, antennas)
        few = dot(choose_few, window).astype(bf16)
        wide = dot_t(channel_ref[g], window).astype(bf16)
        wide_few = dot_t(few, window).astype(bf16)
        out_ref[g, :user_rows] = dot(wide, choose).astype(bf16)
        out_ref[g, user_rows:] = dot(wide_few, choose).astype(bf16)


def make_columns(gathered, channels, place, few):
    groups, user_rows, antennas = channels.shape
    return pl.pallas_call(
        columns_kernel,
        out_shape=jax.ShapeDtypeStruct((groups + 1, user_rows + SHARE_PAD, TOTAL), bf16),
        in_specs=[ANY, VMEM, VMEM, VMEM],
        out_specs=VMEM,
        scratch_shapes=[
            pltpu.VMEM((groups, 16, WINDOW, antennas), bf16),
            pltpu.SemaphoreType.DMA((groups,)),
        ],
        compiler_params=params(),
        cost_estimate=cost(4_000_000_000, 12_000_000),
        name="columns",
    )(gathered, channels, place, few)


def channel_kernel(first_ref, gathered_ref, channel_ref, place_ref, slots_ref, out_ref, window_ref, sems):
    groups, user_rows, antennas = channel_ref.shape
    copies = start_windows(gathered_ref, window_ref, sems, groups, 2 * EPOCHS * 6)
    for g in range(groups):
        here = placing(slots_ref.at[g], first_ref[0], user_rows).astype(bf16)
        route = dot_t(here, choosing(place_ref, g)).astype(bf16)
        copies[g].wait()
        window = window_ref[g].reshape(16 * WINDOW, antennas)
        out_ref[g] = channel_ref[g] + dot(route, window).astype(bf16)


def make_channel(first, gathered, channels, place, slots_mine):
    groups, user_rows, antennas = channels.shape
    return pl.pallas_call(
        channel_kernel,
        out_shape=jax.ShapeDtypeStruct(channels.shape, bf16),
        in_specs=[SMEM, ANY, VMEM, VMEM, VMEM],
        out_specs=VMEM,
        scratch_shapes=[
            pltpu.VMEM((groups, 16, WINDOW, antennas), bf16),
            pltpu.SemaphoreType.DMA((groups,)),
        ],
        compiler_params=params(),
        cost_estimate=cost(4_000_000_000, 14_000_000),
        name="channel",
    )(first, gathered, channels, place, slots_mine)


def middle_kernel(
    where_ref, square_ref, own_ref, row1_ref, row2_ref, row3_ref, col1_ref, col2_ref, col3_ref,
    columns_ref, precoded_ref, slots_ref, first_out, block1_out, block2_out, block3_out, packed_out,
):
    y, x, first = where_ref[0], where_ref[1], where_ref[2]
    user_rows = own_ref.shape[0]
    by_row = [own_ref, row1_ref, row2_ref, row3_ref]
    by_col = [own_ref, col1_ref, col2_ref, col3_ref]
    outs = [first_out, block1_out, block2_out, block3_out]
    schur = None
    for d in range(4):
        rows = pl.ds(pl.multiple_of((x + d) % 4 * user_rows, user_rows), user_rows)
        block = dot(square_ref[y, rows, :], own_ref[...])
        for e in range(1, 4):
            block += dot(square_ref[(y + e) % 4, rows, :], by_col[e][...])
        low = block.astype(bf16)
        outs[d][...] = block if d == 0 else low
        part = t_dot(by_row[d][...], low)
        schur = part if d == 0 else schur + part
    packed_out[:, :TOTAL] = schur.astype(bf16)
    border = columns_ref[...] - placing(slots_ref, first, user_rows)
    packed_out[:, TOTAL:] = split(t_dot, border, precoded_ref[...]).astype(bf16)


def make_middle(where, square, by_row, by_col, columns, precoded, slot_plane):
    shape = columns.shape
    return pl.pallas_call(
        middle_kernel,
        out_shape=(
            jax.ShapeDtypeStruct(shape, f32),
            jax.ShapeDtypeStruct(shape, bf16),
            jax.ShapeDtypeStruct(shape, bf16),
            jax.ShapeDtypeStruct(shape, bf16),
            jax.ShapeDtypeStruct((TOTAL, TOTAL + STREAMS), bf16),
        ),
        in_specs=[SMEM] + [VMEM] * 11,
        out_specs=(VMEM,) * 5,
        compiler_params=params(),
        cost_estimate=cost(2_000_000_000, 8_000_000),
        name="middle",
    )(where, square, *by_row, *by_col[1:], columns, precoded, slot_plane)


def invert_block(a):
    lane = lax.broadcasted_iota(jnp.int32, (1, BLOCK), 1)
    sub = lax.broadcasted_iota(jnp.int32, (PANEL, 1), 0)
    for k in range(0, BLOCK, PANEL):
        inside = (lane >= k) & (lane < k + PANEL)
        rows = a[k:k + PANEL, :]
        cols = [
            jnp.broadcast_to(rows[:, k + j:k + j + 1], (PANEL, BLOCK)) for j in range(PANEL)
        ]
        rows = jnp.where(inside, (lane - k == sub).astype(f32), rows)
        for i in range(PANEL):
            scale = 1.0 / cols[i][i:i + 1, :]
            factor = cols[i] - (sub == i).astype(f32)
            for j in range(i + 1, PANEL):
                cols[j] = cols[j] - factor * (cols[j][i:i + 1, :] * scale)
            rows = rows - factor * (rows[i:i + 1, :] * scale)
        rest = jnp.where(inside, 0.0, a)
        for i in range(PANEL):
            rest = rest - a[:, k + i:k + i + 1] * rows[i:i + 1, :]
        pieces = [rest[:k]] if k else []
        pieces.append(rows)
        if k + PANEL < BLOCK:
            pieces.append(rest[k + PANEL:])
        a = jnp.concatenate(pieces, axis=0)
    return a


def solve_kernel(first_ref, whole_ref, weighted_ref, precoded_ref, slots_ref, inv_ref, users_ref):
    inv_ref[...] = whole_ref[:, :TOTAL]

    @pl.loop(0, TOTAL // BLOCK)
    def _(b):
        start = pl.multiple_of(b * BLOCK, BLOCK)
        here = pl.ds(start, BLOCK)
        pivot_inv = invert_block(inv_ref[here, here])
        panel = inv_ref[:, here]
        row_id = lax.broadcasted_iota(jnp.int32, (TOTAL, BLOCK), 0)
        lane_id = lax.broadcasted_iota(jnp.int32, (TOTAL, BLOCK), 1)
        unit = (row_id == lane_id + start).astype(f32)
        inv_ref[:, here] = unit
        rows = inv_ref[here, :]
        scaled = split(dot, pivot_inv, rows)
        inside = (row_id >= start) & (row_id < start + BLOCK)
        rest = jnp.where(inside, 0.0, panel)
        inv_ref[here, :] = jnp.zeros((BLOCK, TOTAL), f32)
        inv_ref[...] = inv_ref[...] - split(dot, rest, scaled)
        inv_ref[here, :] = scaled

    effect = split(dot, inv_ref[...], whole_ref[:, TOTAL:])
    place = placing(slots_ref, first_ref[0], weighted_ref.shape[0])
    kept = 1.0 - jnp.sum(place, axis=1, keepdims=True)
    users = precoded_ref[...] * kept + split(dot, weighted_ref[...] - place, effect)
    for z in range(4):
        users_ref[z] = users.astype(bf16)


def make_solve(first, whole, weighted, precoded, slot_plane):
    return pl.pallas_call(
        solve_kernel,
        out_shape=(
            jax.ShapeDtypeStruct((TOTAL, TOTAL), f32),
            jax.ShapeDtypeStruct((4, weighted.shape[0], STREAMS), bf16),
        ),
        in_specs=[SMEM] + [VMEM] * 4,
        out_specs=(VMEM,) * 2,
        compiler_params=params(),
        cost_estimate=cost(10_000_000_000, 4_000_000),
        name="solve",
    )(first, whole, weighted, precoded, slot_plane)


def signal_kernel(users_ref, channel_ref, out_ref):
    part = t_dot(users_ref[0], channel_ref[0]).astype(bf16)
    out_ref[...] = part.reshape(out_ref.shape)


def make_signal(users_side, channel):
    groups, user_rows, antennas = channel.shape
    tile = 1024
    each = STREAMS // 16
    return pl.pallas_call(
        signal_kernel,
        out_shape=jax.ShapeDtypeStruct((16, groups, each, antennas), bf16),
        grid=(groups, antennas // tile),
        in_specs=[
            pl.BlockSpec((1, user_rows, STREAMS), lambda g, m: (g, 0, 0)),
            pl.BlockSpec((1, user_rows, tile), lambda g, m: (g, 0, m)),
        ],
        out_specs=pl.BlockSpec((16, 1, each, tile), lambda g, m: (0, g, 0, m)),
        compiler_params=params(),
        cost_estimate=cost(800_000_000, 7_000_000),
        name="signal",
    )(users_side, channel)


def update_kernel(first_ref, weighted_ref, inv_ref, all_ref, slots_ref, out_ref):
    user_rows = weighted_ref.shape[0]
    border = weighted_ref[...] - placing(slots_ref, first_ref[0], user_rows)
    half = split(dot, border, inv_ref[...]).astype(bf16)
    for z in range(4):
        there = all_ref[4 * z:4 * z + 4].reshape(4 * user_rows, TOTAL).astype(f32)
        there = there - placing(slots_ref, 4 * user_rows * z, 4 * user_rows)
        out_ref[z] = dot_t(half, there.astype(bf16)).astype(bf16)


def make_update(first, weighted, schur_inverse, weighted_all, slot_plane):
    user_rows = weighted.shape[0]
    return pl.pallas_call(
        update_kernel,
        out_shape=jax.ShapeDtypeStruct((4, user_rows, 4 * user_rows), bf16),
        in_specs=[SMEM] + [VMEM] * 4,
        out_specs=VMEM,
        compiler_params=params(),
        cost_estimate=cost(1_500_000_000, 8_000_000),
        name="update",
    )(first, weighted, schur_inverse, weighted_all, slot_plane)


def local(channels, inverse, arrivals, arrival_cell, cell_owner, slots, symbols):
    group_count, user_rows, antennas = channels.shape
    user_cols = inverse.shape[2]
    capacity = arrivals.shape[2]
    cell_count = cell_owner.shape[0]
    grp_index = lax.axis_index("grp")
    row_index = lax.axis_index("row")
    col_index = lax.axis_index("col")
    y_index, x_index = row_index // 4, row_index % 4
    x_groups = [[4 * y + x for x in range(4)] for y in range(4)]

    def along_x(value, step):
        pairs = [(4 * y + x, 4 * y + (x + step) % 4) for y in range(4) for x in range(4)]
        return lax.ppermute(value, "row", pairs)

    def along_y(value, step):
        pairs = [(4 * y + x, 4 * ((y + step) % 4) + x) for y in range(4) for x in range(4)]
        return lax.ppermute(value, "row", pairs)

    def to_planes(value):
        padded = jnp.concatenate([value, jnp.zeros_like(value[:1])], axis=0)
        return lax.all_to_all(padded, "col", 0, 0, tiled=True)

    first_group = grp_index * group_count
    other_first = (1 - grp_index) * group_count
    first_row = row_index * user_rows
    first_arg = first_row.reshape(1)

    with jax.named_scope("newcomers"):
        mine = lax.dynamic_slice_in_dim(arrivals, first_group, group_count, 0)
        theirs = lax.dynamic_slice_in_dim(arrivals, other_first, group_count, 0)
        swapped = lax.ppermute(theirs, "grp", [(0, 1), (1, 0)])
        from_0 = jnp.where(grp_index == 0, mine, swapped)
        from_1 = jnp.where(grp_index == 0, swapped, mine)
        chunk = jnp.stack([from_0, from_1], axis=2)
        per_group = EPOCHS * 2 * capacity
        chunk = chunk.reshape(group_count * per_group, antennas)
        chunk = jnp.pad(chunk, ((0, 112 - group_count * per_group), (0, 0)))
        gathered = lax.all_gather(chunk, "row")

    with jax.named_scope("planes"):
        low = inverse.astype(bf16).reshape(group_count, user_rows, 4, user_rows)
        by_x = low.transpose(2, 0, 1, 3)
        by_x = lax.all_to_all(by_x, "row", 0, 0, axis_index_groups=x_groups, tiled=True)
        by_group = by_x.transpose(1, 0, 2, 3).reshape(group_count, 4 * user_rows, user_rows)
        square = to_planes(by_group)
        symbol_part = jnp.einsum(
            "grc,gcs->grs", inverse, symbols.astype(f32), precision=highest
        )
        precoded = jnp.sum(to_planes(symbol_part), axis=0)

    plane_group = first_group + jnp.minimum(col_index, group_count - 1)
    slot_plane = lax.dynamic_slice_in_dim(slots, plane_group, 1, 0).reshape(1, TOTAL)
    row_ids = first_row + jnp.arange(user_rows, dtype=jnp.int32)

    cells_mine = lax.dynamic_slice_in_dim(arrival_cell, first_group, group_count, 0)[..., 0]
    slots_mine = lax.dynamic_slice_in_dim(slots, first_group, group_count, 0)
    slots_mine = slots_mine.reshape(group_count, 1, TOTAL)
    cell_table = (cells_mine[..., None] == jnp.arange(cell_count, dtype=jnp.int32)).astype(
        jnp.int32
    )
    owners = jnp.sum(cell_table * cell_owner, axis=-1)
    arrival_order = jnp.arange(ARRIVE, dtype=jnp.int32)
    earlier = (cells_mine[..., :, None] == cells_mine[..., None, :]) & (
        arrival_order[:, None] < arrival_order[None, :]
    )
    ranking = jnp.sum(earlier.astype(jnp.int32), axis=-2)
    with jax.named_scope("places"):
        offset = jnp.arange(group_count, dtype=jnp.int32) * per_group % 16
        epoch = jnp.arange(EPOCHS, dtype=jnp.int32)
        inside = offset[:, None] + epoch[None, :] * 2 * capacity
        inside = inside[:, :, None] + owners // 16 * capacity + ranking
        place = (owners % 16 * WINDOW + inside).reshape(group_count, 1, TOTAL)
        few = lax.dynamic_slice_in_dim(place, row_index * SHARE, SHARE, 2)
        few = jnp.pad(few, ((0, 0), (0, 0), (0, SHARE_PAD - SHARE)), constant_values=-1)
        few = few.reshape(group_count, SHARE_PAD, 1)

    with jax.named_scope("columns"):
        gathered, square, precoded = lax.optimization_barrier((gathered, square, precoded))
        both = make_columns(gathered, channels, place, few)
        both = lax.all_to_all(both, "col", 0, 0, tiled=True)
        summed = jnp.sum(both.astype(f32), axis=0)
        columns = summed[:user_rows]
        gram = summed[user_rows:user_rows + SHARE]
        own = columns.astype(bf16)
        by_row = [own] + [along_x(own, -d) for d in (1, 2, 3)]
        by_col = [own] + [along_y(own, -d) for d in (1, 2, 3)]

    with jax.named_scope("schur"):
        where = jnp.stack([y_index, x_index, first_row])
        block0, block1, block2, block3, packed = make_middle(
            where, square, by_row, by_col, columns, precoded, slot_plane
        )
        weighted = block0
        for d, block in ((1, block1), (2, block2), (3, block3)):
            weighted = weighted + along_x(block, d).astype(f32)
        packed = packed.reshape(16, SHARE, TOTAL + STREAMS)
        shared = lax.all_to_all(packed, "row", 0, 0, tiled=True).astype(f32)
        shared = jnp.sum(shared, axis=0)
        share_ids = row_index * SHARE + jnp.arange(SHARE, dtype=jnp.int32)
        identity = loading * (
            share_ids[:, None] == jnp.arange(TOTAL, dtype=jnp.int32)[None, :]
        ).astype(f32)
        schur_rows = gram + identity - shared[:, :TOTAL]
        ready = jnp.concatenate([schur_rows, shared[:, TOTAL:]], axis=1)
        ready = jnp.broadcast_to(ready[None], (16, SHARE, TOTAL + STREAMS))
        whole = lax.all_to_all(ready, "row", 0, 0, tiled=True).reshape(TOTAL, TOTAL + STREAMS)

    with jax.named_scope("users"):
        weighted_all = lax.all_gather(weighted.astype(bf16), "row")
        channel = make_channel(first_arg, gathered, channels, place, slots_mine)
        schur_inverse, users = make_solve(first_arg, whole, weighted, precoded, slot_plane)
        users_side = lax.all_to_all(users, "col", 0, 0, tiled=True)

    with jax.named_scope("update"):
        change = make_update(first_arg, weighted, schur_inverse, weighted_all, slot_plane)
        change = lax.all_to_all(change, "col", 0, 0, tiled=True)

    with jax.named_scope("signal"):
        signal_part = make_signal(users_side, channel)
        received = lax.all_to_all(signal_part, "row", 0, 0, tiled=True)
        received, change = lax.optimization_barrier((received, change))
        signal = jnp.sum(received.astype(f32), axis=0)
        power = jnp.sum(signal * signal, axis=(1, 2))
        power = jnp.broadcast_to(power[None, None, :], (64, 1, group_count))
        power = lax.all_to_all(power, ("row", "col"), 0, 0, tiled=True)
        total_power = jnp.sum(power, axis=(0, 1)) / (STREAMS * ANTENNAS)
        transmit = signal * lax.rsqrt(total_power + epsilon)[:, None, None]
        transmit = jnp.swapaxes(transmit, 0, 1)

    with jax.named_scope("final"):
        col_ids = col_index * user_cols + jnp.arange(user_cols, dtype=jnp.int32)
        diagonal = row_ids[:, None] == col_ids[None, :]
        full = jnp.any(slots_mine == row_ids[None, :, None], axis=2)
        gone = jnp.where(diagonal[None] & full[:, :, None], 1.0 / loading, 0.0)
        updated = inverse - gone + change[:group_count].astype(f32)
    return (updated, transmit)


def solution(mesh):
    placed = (
        P("grp", "row", "col"),
        P("grp", "row", "col"),
        P(None, None, ("grp", "row"), "col"),
        P(),
        P(),
        P(),
        P("grp", "col", None),
    )
    return jax.shard_map(
        local,
        mesh=mesh,
        in_specs=placed,
        out_specs=(P("grp", "row", "col"), P("row", "grp", "col")),
        check_vma=False,
    )
```

profile of v0, /device:TPU:0, one launch (start us, length us, event | category | flops | bytes accessed | tf_op | source)
XLA Modules:
  0.0 308.7 jit_solution(3072316336940891751)
XLA Ops:
  7.2 1.1 constant_dynamic-slice_fusion.2
  8.4 1.6 collective-permute-done
  10.0 1.0 select_bitcast_fusion.1
  11.3 0.8 pad.10
  12.2 2.2 copy.34
  14.4 1.6 copy.35
  15.9 4.4 %all-to-all-start = ((bf16[4,3,256,256]{3,2,1,0:T(8,128)(2,1)}), bf16[4,3,256,256]{3,2,1,0:T(8,128)(2,1)S(1)}, u32[]{:S(2)}, u32[]{:S(2)}) async-start(bf16[4,3,256,256]{3,2,1,0:T(8,128)(2,1)} %copy.35), calls=%async_computation | async-start | bytes 3145728 | tf_op jit(solution)/shard_map/planes/all_to_all | solution.py:348
  20.3 3.5 %fusion.4 = f32[3,256,256]{2,1,0:T(8,128)S(1)} fusion(f32[3,256,1024]{2,1,0:T(8,128)} %param.8, bf16[3,1024,256]{2,1,0:T(8,128)(2,1)S(1)} %copy-done), kind=kOutput, calls=%fused_computation.49 | convolution fusion | flops 2415919104 | bytes 5505024 | tf_op jit(solution)/shard_map/planes/grc,gcs->grs/dot_general | solution.py:351
  23.8 1.2 concatenate.10
  25.0 23.7 %all-to-all-done = bf16[4,3,256,256]{3,2,1,0:T(8,128)(2,1)S(1)} async-done(((bf16[4,3,256,256]{3,2,1,0:T(8,128)(2,1)}), bf16[4,3,256,256]{3,2,1,0:T(8,128)(2,1)S(1)}, u32[]{:S(2)}, u32[]{:S(2)}) %all-to-all-start) | async-done | bytes 1572896 | tf_op jit(solution)/shard_map/planes/all_to_all | solution.py:348
  48.7 5.3 %all-to-all-start.2 = ((f32[4,256,256]{2,1,0:T(8,128)}), f32[4,256,256]{2,1,0:T(8,128)}, u32[]{:S(2)}, u32[]{:S(2)}) async-start(f32[4,256,256]{2,1,0:T(8,128)} %concatenate.10), calls=%async_computation.2 | async-start | bytes 2097152 | tf_op jit(solution)/shard_map/planes/all_to_all | solution.py:326
  54.1 1.5 concatenate.9
  55.6 12.8 %all-to-all-done.2 = f32[4,256,256]{2,1,0:T(8,128)} async-done(((f32[4,256,256]{2,1,0:T(8,128)}), f32[4,256,256]{2,1,0:T(8,128)}, u32[]{:S(2)}, u32[]{:S(2)}) %all-to-all-start.2) | async-done | bytes 1048608 | tf_op jit(solution)/shard_map/planes/all_to_all | solution.py:326
  68.4 4.5 %all-to-all-start.1 = ((bf16[4,1024,256]{2,1,0:T(8,128)(2,1)}), bf16[4,1024,256]{2,1,0:T(8,128)(2,1)}, u32[]{:S(2)}, u32[]{:S(2)}) async-start(bf16[4,1024,256]{2,1,0:T(8,128)(2,1)} %concatenate.9), calls=%async_computation.1 | async-start | bytes 4194304 | tf_op jit(solution)/shard_map/planes/all_to_all | solution.py:326
  73.7 1.4 reduce_sum.76.precoded_ref
  75.1 22.4 %all-to-all-done.1.square_ref = bf16[4,1024,256]{2,1,0:T(8,128)(2,1)} async-done(((bf16[4,1024,256]{2,1,0:T(8,128)(2,1)}), bf16[4,1024,256]{2,1,0:T(8,128)(2,1)}, u32[]{:S(2)}, u32[]{:S(2)}) %all-to-all-start.1) | async-done | bytes 2097184 | tf_op jit(solution)/shard_map/planes/all_to_all | solution.py:326
  97.5 3.1 copy-done.7
  100.6 1.9 copy-done.9
  102.4 9.2 %columns.1 = bf16[4,288,384]{2,1,0:T(8,128)(2,1)S(1)} custom-call(bf16[16,112,2048]{2,1,0:T(8,128)(2,1)S(1)} %bitcast.40, bf16[3,256,2048]{2,1,0:T(8,128)(2,1)S(1)} %copy-done.9, s32[3,1,384]{2,1,0:T(1,128)S(1)} %fusion.1.place_ref, s32[3,32,1]{2,1,0:T(8,128)S(1)} %copy.37.few_ref), custom_call_target="tpu_custom_call" | custom-call | flops 4000000000 | bytes 12000000 | tf_op jit(solution)/shard_map/columns/columns/pallas_call | solution.py:101
  111.7 13.1 %all_to_all.50 = bf16[4,288,384]{2,1,0:T(8,128)(2,1)S(1)} all-to-all(bf16[4,288,384]{2,1,0:T(8,128)(2,1)S(1)} %columns.1), channel_id=1, replica_groups=mesh['grp'=2,'row'=16,'col'=4] {'col'}, dimensions={0} | all-to-all | bytes 1769472 | tf_op jit(solution)/shard_map/columns/all_to_all | solution.py:385
  124.9 0.8 copy-done.13
  125.7 1.2 collective-permute-start.1
  126.9 1.4 collective-permute-start.2
  128.3 3.0 collective-permute-start.4
  132.0 1.0 collective-permute-start.6
  133.1 1.0 slice.21.columns_ref
  134.2 2.0 collective-permute-done.3.row3_ref
  136.7 2.0 collective-permute-done.5.col2_ref
  138.6 2.0 collective-permute-done.6.col3_ref
  141.3 0.9 copy-done.12
  142.2 4.5 %middle.1 = (f32[256,384]{1,0:T(8,128)S(1)}, bf16[256,384]{1,0:T(8,128)(2,1)}, bf16[256,384]{1,0:T(8,128)(2,1)}, bf16[256,384]{1,0:T(8,128)(2,1)}, bf16[384,640]{1,0:T(8,128)(2,1)}) custom-call(s32[3]{0:T(128)S(1)} %pad_add_fusion.where_ref, bf16[4,1024,256]{2,1,0:T(8,128)(2,1)} %all-to-all-done.1.square_ref, bf16[256,384]{1,0:T(8,128)(2,1)S(1)} %slice.30.own_ref, ...), custom_call_target="tpu_custom_call" | custom-call | flops 2000000000 | bytes 8000000 | tf_op jit(solution)/shard_map/schur/middle/pallas_call | solution.py:170
  146.7 3.2 %collective-permute-start.9 = (bf16[256,384]{1,0:T(8,128)(2,1)}, bf16[256,384]{1,0:T(8,128)(2,1)S(1)}, u32[]{:S(2)}, u32[]{:S(2)}) collective-permute-start(bf16[256,384]{1,0:T(8,128)(2,1)} %get-tuple-element.21), channel_id=1, source_target_pairs={{0,12},{4,0},{8,4},{12,8},{16,28},{20,16},{24,20},{28,24},{32,44},... | collective-permute-start | bytes 589832 | tf_op jit(solution)/shard_map/schur/ppermute | solution.py:318
  149.9 0.9 collective-permute-start.8
  150.8 0.8 collective-permute-start.7
  151.7 3.8 %all-to-all-start.4 = ((bf16[16,24,640]{2,1,0:T(8,128)(2,1)}), bf16[16,24,640]{2,1,0:T(8,128)(2,1)S(1)}, u32[]{:S(2)}, u32[]{:S(2)}) async-start(bf16[16,24,640]{2,1,0:T(8,128)(2,1)} %bitcast.11), calls=%async_computation.4 | async-start | bytes 983040 | tf_op jit(solution)/shard_map/schur/all_to_all | solution.py:402
  155.6 1.9 collective-permute-done.8
  157.5 2.0 collective-permute-done.7
  159.5 0.7 copy-done.15
  160.2 1.8 fusion.3
  162.0 3.5 %all-to-all-done.4 = bf16[16,24,640]{2,1,0:T(8,128)(2,1)S(1)} async-done(((bf16[16,24,640]{2,1,0:T(8,128)(2,1)}), bf16[16,24,640]{2,1,0:T(8,128)(2,1)S(1)}, u32[]{:S(2)}, u32[]{:S(2)}) %all-to-all-start.4) | async-done | bytes 491552 | tf_op jit(solution)/shard_map/schur/all_to_all | solution.py:402
  165.6 0.8 slice_subtract_fusion
  166.5 16.9 %all_to_all.51 = f32[16,24,640]{2,1,0:T(8,128)S(1)} all-to-all(f32[16,24,640]{2,1,0:T(8,128)S(1)} %broadcast_in_dim.12), channel_id=1, replica_groups=mesh['grp'=2,'row'=16,'col'=4] {'row'}, dimensions={0} | all-to-all | bytes 1966080 | tf_op jit(solution)/shard_map/schur/all_to_all | solution.py:411
  183.4 13.9 %solve.1 = (f32[384,384]{1,0:T(8,128)S(1)}, bf16[4,256,256]{2,1,0:T(8,128)(2,1)S(1)}) custom-call(s32[1]{0:T(128)} %bitcast.first_ref, f32[384,640]{1,0:T(8,128)S(1)} %bitcast.36, f32[256,384]{1,0:T(8,128)S(1)} %get-tuple-element.27.weighted_ref, f32[256,256]{1,0:T(8,128)S(1)} %reduce_sum.76.precoded_ref, s32[1,384]{1,0:T(1,128)S(1)} %bitcast.38), custom_call_target="tpu_custom_call" | custom-call | flops 10000000000 | bytes 4000000 | tf_op jit(solution)/shard_map/users/solve/pallas_call | solution.py:244
  197.3 0.8 copy-done.6
  198.2 3.7 %all-to-all-start.6 = ((bf16[4,256,256]{2,1,0:T(8,128)(2,1)}), bf16[4,256,256]{2,1,0:T(8,128)(2,1)S(1)}, u32[]{:S(2)}, u32[]{:S(2)}) async-start(bf16[4,256,256]{2,1,0:T(8,128)(2,1)} %copy-done.6), calls=%async_computation.6 | async-start | bytes 1048576 | tf_op jit(solution)/shard_map/users/all_to_all | solution.py:417
  201.9 3.2 %copy-done.8 = bf16[1792,2048]{1,0:T(8,128)(2,1)S(1)} copy-done((bf16[1792,2048]{1,0:T(8,128)(2,1)S(1)}, bf16[1792,2048]{1,0:T(8,128)(2,1)}, u32[]{:S(2)}) %copy-start.8) | copy-done | bytes 7340056
  205.1 1.9 copy-done.10
  207.0 4.6 %channel.1.channel_ref = bf16[3,256,2048]{2,1,0:T(8,128)(2,1)S(1)} custom-call(s32[1]{0:T(128)} %bitcast.first_ref, bf16[16,112,2048]{2,1,0:T(8,128)(2,1)S(1)} %bitcast.41, bf16[3,256,2048]{2,1,0:T(8,128)(2,1)S(1)} %copy-done.10, s32[3,1,384]{2,1,0:T(1,128)S(1)} %fusion.1.place_ref, s32[3,1,384]{2,1,0:T(1,128)S(1)} %reshape.281.slots_ref), custom_call_target="tpu_custom_call" | custom-call | flops 4000000000 | bytes 14000000 | tf_op jit(solution)/shard_map/users/channel/pallas_call | solution.py:129
  211.6 1.7 copy-done.4
  213.3 1.9 copy-done.5
  215.2 2.4 signal.1
  217.6 1.7 copy-done.1
  219.3 4.5 %all-to-all-start.7 = ((bf16[16,3,16,2048]{3,2,1,0:T(8,128)(2,1)}), bf16[16,3,16,2048]{3,2,1,0:T(8,128)(2,1)}, u32[]{:S(2)}, u32[]{:S(2)}) async-start(bf16[16,3,16,2048]{3,2,1,0:T(8,128)(2,1)} %copy-done.1), calls=%async_computation.7 | async-start | bytes 6291456 | tf_op jit(solution)/shard_map/signal/all_to_all | solution.py:425
  223.8 1.9 copy-done.3
  225.7 1.8 update.1
  227.5 1.3 copy-done.2
  228.8 31.5 %all-to-all-done.7 = bf16[16,3,16,2048]{3,2,1,0:T(8,128)(2,1)} async-done(((bf16[16,3,16,2048]{3,2,1,0:T(8,128)(2,1)}), bf16[16,3,16,2048]{3,2,1,0:T(8,128)(2,1)}, u32[]{:S(2)}, u32[]{:S(2)}) %all-to-all-start.7) | async-done | bytes 3145760 | tf_op jit(solution)/shard_map/signal/all_to_all | solution.py:425
  260.3 4.5 %all-to-all-start.8 = ((bf16[4,256,1024]{2,1,0:T(8,128)(2,1)}), bf16[4,256,1024]{2,1,0:T(8,128)(2,1)}, u32[]{:S(2)}, u32[]{:S(2)}) async-start(bf16[4,256,1024]{2,1,0:T(8,128)(2,1)} %copy-done.2), calls=%async_computation.8 | async-start | bytes 4194304 | tf_op jit(solution)/shard_map/update/all_to_all | solution.py:421
  265.3 16.6 %all-to-all-done.8 = bf16[4,256,1024]{2,1,0:T(8,128)(2,1)} async-done(((bf16[4,256,1024]{2,1,0:T(8,128)(2,1)}), bf16[4,256,1024]{2,1,0:T(8,128)(2,1)}, u32[]{:S(2)}, u32[]{:S(2)}) %all-to-all-start.8) | async-done | bytes 2097184 | tf_op jit(solution)/shard_map/update/all_to_all | solution.py:421
  281.9 2.5 convert_reduce_fusion
  285.3 6.2 %all-to-all-start.9 = ((f32[64,1,3]{2,1,0:T(1,128)}), f32[64,1,3]{2,1,0:T(1,128)S(1)}, u32[]{:S(2)}, u32[]{:S(2)}) async-start(f32[64,1,3]{2,1,0:T(1,128)} %broadcast_in_dim.13), calls=%async_computation.9 | async-start | bytes 65536 | tf_op jit(solution)/shard_map/signal/all_to_all | solution.py:430
  291.4 4.7 %convert_add_fusion = f32[3,256,1024]{2,1,0:T(8,128)} fusion(f32[3,256,1024]{2,1,0:T(8,128)} %param.8, bf16[4,256,1024]{2,1,0:T(8,128)(2,1)} %all-to-all-done.8, pred[3,256]{1,0:T(4,128)(4,1)S(1)} %compare_reduce_fusion, pred[256,1024]{1,0:T(8,128)(4,1)S(1)} %broadcast_compare_fusion), kind=kLoop, calls=%fused_computation.1 | loop fusion | flops 3932160 | bytes 8127232 | tf_op jit(solution)/shard_map/final/add | solution.py:440
  296.2 4.7 %all-to-all-done.9 = f32[64,1,3]{2,1,0:T(1,128)S(1)} async-done(((f32[64,1,3]{2,1,0:T(1,128)}), f32[64,1,3]{2,1,0:T(1,128)S(1)}, u32[]{:S(2)}, u32[]{:S(2)}) %all-to-all-start.9) | async-done | bytes 800 | tf_op jit(solution)/shard_map/signal/all_to_all | solution.py:430
  301.0 0.8 multiply_bitcast_fusion
  (80 shorter events, 5.2 us)
Async XLA Ops:
  7.2 13.2 %copy-start = (bf16[3,1024,256]{2,1,0:T(8,128)(2,1)S(1)}, bf16[3,1024,256]{2,1,0:T(8,128)(2,1)}, u32[]{:S(2)}) copy-start(bf16[3,1024,256]{2,1,0:T(8,128)(2,1)} %param.13) | copy-start | bytes 4718596
  7.2 90.3 %all-gather.5.cloned.1.call-start = ((), (), s32[]{:S(2)}) async-start(), calls=%async_computation.10 | async-start | bytes 7798784 | tf_op jit(solution)/shard_map/newcomers/all_gather | solution.py:343
  8.3 1.7 collective-permute-start
  15.9 32.8 %all-to-all-start = ((bf16[4,3,256,256]{3,2,1,0:T(8,128)(2,1)}), bf16[4,3,256,256]{3,2,1,0:T(8,128)(2,1)S(1)}, u32[]{:S(2)}, u32[]{:S(2)}) async-start(bf16[4,3,256,256]{3,2,1,0:T(8,128)(2,1)} %copy.35), calls=%async_computation | async-start | bytes 3145728 | tf_op jit(solution)/shard_map/planes/all_to_all | solution.py:348
  48.7 19.7 %all-to-all-start.2 = ((f32[4,256,256]{2,1,0:T(8,128)}), f32[4,256,256]{2,1,0:T(8,128)}, u32[]{:S(2)}, u32[]{:S(2)}) async-start(f32[4,256,256]{2,1,0:T(8,128)} %concatenate.10), calls=%async_computation.2 | async-start | bytes 2097152 | tf_op jit(solution)/shard_map/planes/all_to_all | solution.py:326
  54.1 18.7 %copy-start.17 = (s32[6,3,128,1]{2,3,1,0:T(1,128)S(1)}, s32[6,3,128,1]{2,3,1,0:T(1,128)}, u32[]{:S(2)}) copy-start(s32[6,3,128,1]{2,3,1,0:T(1,128)} %param.10) | copy-start | bytes 27652
  54.1 19.2 %copy-start.18 = (s32[32]{0:T(128)S(1)}, s32[32]{0:T(128)}, u32[]{:S(2)}) copy-start(s32[32]{0:T(128)} %param.11) | copy-start | bytes 388
  68.4 29.1 %all-to-all-start.1 = ((bf16[4,1024,256]{2,1,0:T(8,128)(2,1)}), bf16[4,1024,256]{2,1,0:T(8,128)(2,1)}, u32[]{:S(2)}, u32[]{:S(2)}) async-start(bf16[4,1024,256]{2,1,0:T(8,128)(2,1)} %concatenate.9), calls=%async_computation.1 | async-start | bytes 4194304 | tf_op jit(solution)/shard_map/planes/all_to_all | solution.py:326
  97.5 3.1 copy-start.7
  100.5 1.9 copy-start.9
  111.7 21.3 %copy-start.16 = (s32[6,3,128]{2,1,0:T(4,128)S(1)}, s32[6,3,128]{2,1,0:T(4,128)}, u32[]{:S(2)}) copy-start(s32[6,3,128]{2,1,0:T(4,128)} %param.12) | copy-start | bytes 27652
  124.9 0.8 copy-start.13
  125.7 6.3 %collective-permute-start.1 = (bf16[256,384]{1,0:T(8,128)(2,1)S(1)}, bf16[256,384]{1,0:T(8,128)(2,1)S(1)}, u32[]{:S(2)}, u32[]{:S(2)}) collective-permute-start(bf16[256,384]{1,0:T(8,128)(2,1)S(1)} %slice.30.own_ref), channel_id=1, source_target_pairs={{0,12},{4,0},{8,4},{12,8},{16,28},{20,16},{24,20},{28,24},{32,44},... | collective-permute-start | bytes 589832 | tf_op jit(solution)/shard_map/columns/ppermute | solution.py:318
  126.9 7.3 %collective-permute-start.2 = (bf16[256,384]{1,0:T(8,128)(2,1)S(1)}, bf16[256,384]{1,0:T(8,128)(2,1)S(1)}, u32[]{:S(2)}, u32[]{:S(2)}) collective-permute-start(bf16[256,384]{1,0:T(8,128)(2,1)S(1)} %slice.30.own_ref), channel_id=1, source_target_pairs={{0,8},{4,12},{8,0},{12,4},{16,24},{20,28},{24,16},{28,20},{32,40},... | collective-permute-start | bytes 589832 | tf_op jit(solution)/shard_map/columns/ppermute | solution.py:318
  128.3 7.9 %collective-permute-start.3 = (bf16[256,384]{1,0:T(8,128)(2,1)S(1)}, bf16[256,384]{1,0:T(8,128)(2,1)S(1)}, u32[]{:S(2)}, u32[]{:S(2)}) collective-permute-start(bf16[256,384]{1,0:T(8,128)(2,1)S(1)} %slice.30.own_ref), channel_id=1, source_target_pairs={{0,4},{4,8},{8,12},{12,0},{16,20},{20,24},{24,28},{28,16},{32,36},... | collective-permute-start | bytes 589832 | tf_op jit(solution)/shard_map/columns/ppermute | solution.py:318
  128.3 8.3 %collective-permute-start.4 = (bf16[256,384]{1,0:T(8,128)(2,1)S(1)}, bf16[256,384]{1,0:T(8,128)(2,1)S(1)}, u32[]{:S(2)}, u32[]{:S(2)}) collective-permute-start(bf16[256,384]{1,0:T(8,128)(2,1)S(1)} %slice.30.own_ref), channel_id=1, source_target_pairs={{0,48},{4,52},{8,56},{12,60},{16,0},{20,4},{24,8},{28,12},{32,16},... | collective-permute-start | bytes 589832 | tf_op jit(solution)/shard_map/columns/ppermute | solution.py:322
  131.3 7.3 %collective-permute-start.5 = (bf16[256,384]{1,0:T(8,128)(2,1)S(1)}, bf16[256,384]{1,0:T(8,128)(2,1)S(1)}, u32[]{:S(2)}, u32[]{:S(2)}) collective-permute-start(bf16[256,384]{1,0:T(8,128)(2,1)S(1)} %slice.30.own_ref), channel_id=1, source_target_pairs={{0,32},{4,36},{8,40},{12,44},{16,48},{20,52},{24,56},{28,60},{32,0... | collective-permute-start | bytes 589832 | tf_op jit(solution)/shard_map/columns/ppermute | solution.py:322
  132.0 8.6 %collective-permute-start.6 = (bf16[256,384]{1,0:T(8,128)(2,1)S(1)}, bf16[256,384]{1,0:T(8,128)(2,1)S(1)}, u32[]{:S(2)}, u32[]{:S(2)}) collective-permute-start(bf16[256,384]{1,0:T(8,128)(2,1)S(1)} %slice.30.own_ref), channel_id=1, source_target_pairs={{0,16},{4,20},{8,24},{12,28},{16,32},{20,36},{24,40},{28,44},{32,4... | collective-permute-start | bytes 589832 | tf_op jit(solution)/shard_map/columns/ppermute | solution.py:322
  140.6 0.7 copy-start.11
  141.3 0.9 copy-start.12
  146.7 8.9 %collective-permute-start.9 = (bf16[256,384]{1,0:T(8,128)(2,1)}, bf16[256,384]{1,0:T(8,128)(2,1)S(1)}, u32[]{:S(2)}, u32[]{:S(2)}) collective-permute-start(bf16[256,384]{1,0:T(8,128)(2,1)} %get-tuple-element.21), channel_id=1, source_target_pairs={{0,12},{4,0},{8,4},{12,8},{16,28},{20,16},{24,20},{28,24},{32,44},... | collective-permute-start | bytes 589832 | tf_op jit(solution)/shard_map/schur/ppermute | solution.py:318
  149.9 7.5 %collective-permute-start.8 = (bf16[256,384]{1,0:T(8,128)(2,1)}, bf16[256,384]{1,0:T(8,128)(2,1)S(1)}, u32[]{:S(2)}, u32[]{:S(2)}) collective-permute-start(bf16[256,384]{1,0:T(8,128)(2,1)} %get-tuple-element.20), channel_id=1, source_target_pairs={{0,8},{4,12},{8,0},{12,4},{16,24},{20,28},{24,16},{28,20},{32,40},... | collective-permute-start | bytes 589832 | tf_op jit(solution)/shard_map/schur/ppermute | solution.py:318
  150.8 8.6 %collective-permute-start.7 = (bf16[256,384]{1,0:T(8,128)(2,1)}, bf16[256,384]{1,0:T(8,128)(2,1)S(1)}, u32[]{:S(2)}, u32[]{:S(2)}) collective-permute-start(bf16[256,384]{1,0:T(8,128)(2,1)} %get-tuple-element.19), channel_id=1, source_target_pairs={{0,4},{4,8},{8,12},{12,0},{16,20},{20,24},{24,28},{28,16},{32,36},... | collective-permute-start | bytes 589832 | tf_op jit(solution)/shard_map/schur/ppermute | solution.py:318
  151.7 13.8 %all-to-all-start.4 = ((bf16[16,24,640]{2,1,0:T(8,128)(2,1)}), bf16[16,24,640]{2,1,0:T(8,128)(2,1)S(1)}, u32[]{:S(2)}, u32[]{:S(2)}) async-start(bf16[16,24,640]{2,1,0:T(8,128)(2,1)} %bitcast.11), calls=%async_computation.4 | async-start | bytes 983040 | tf_op jit(solution)/shard_map/schur/all_to_all | solution.py:402
  155.5 68.2 %all-gather.7.cloned.1.call-start = ((), (), s32[]{:S(2)}) async-start(), calls=%async_computation.11 | async-start | bytes 3342336 | tf_op jit(solution)/shard_map/users/all_gather | solution.py:414
  157.5 2.0 copy-start.14
  159.5 0.7 copy-start.15
  197.3 0.8 copy-start.6
  198.2 15.1 %all-to-all-start.6 = ((bf16[4,256,256]{2,1,0:T(8,128)(2,1)}), bf16[4,256,256]{2,1,0:T(8,128)(2,1)S(1)}, u32[]{:S(2)}, u32[]{:S(2)}) async-start(bf16[4,256,256]{2,1,0:T(8,128)(2,1)} %copy-done.6), calls=%async_computation.6 | async-start | bytes 1048576 | tf_op jit(solution)/shard_map/users/all_to_all | solution.py:417
  201.9 3.2 %copy-start.8 = (bf16[1792,2048]{1,0:T(8,128)(2,1)S(1)}, bf16[1792,2048]{1,0:T(8,128)(2,1)}, u32[]{:S(2)}) copy-start(bf16[1792,2048]{1,0:T(8,128)(2,1)} %all-gather.5.cloned.1.call-done) | copy-start | bytes 22020100
  205.1 1.9 copy-start.10
  211.6 1.7 copy-start.4
  213.3 1.9 copy-start.5
  217.6 1.7 copy-start.1
  219.3 41.1 %all-to-all-start.7 = ((bf16[16,3,16,2048]{3,2,1,0:T(8,128)(2,1)}), bf16[16,3,16,2048]{3,2,1,0:T(8,128)(2,1)}, u32[]{:S(2)}, u32[]{:S(2)}) async-start(bf16[16,3,16,2048]{3,2,1,0:T(8,128)(2,1)} %copy-done.1), calls=%async_computation.7 | async-start | bytes 6291456 | tf_op jit(solution)/shard_map/signal/all_to_all | solution.py:425
  223.8 1.9 copy-start.3
  227.4 1.3 copy-start.2
  260.3 21.6 %all-to-all-start.8 = ((bf16[4,256,1024]{2,1,0:T(8,128)(2,1)}), bf16[4,256,1024]{2,1,0:T(8,128)(2,1)}, u32[]{:S(2)}, u32[]{:S(2)}) async-start(bf16[4,256,1024]{2,1,0:T(8,128)(2,1)} %copy-done.2), calls=%async_computation.8 | async-start | bytes 4194304 | tf_op jit(solution)/shard_map/update/all_to_all | solution.py:421
  285.3 15.7 %all-to-all-start.9 = ((f32[64,1,3]{2,1,0:T(1,128)}), f32[64,1,3]{2,1,0:T(1,128)S(1)}, u32[]{:S(2)}, u32[]{:S(2)}) async-start(f32[64,1,3]{2,1,0:T(1,128)} %broadcast_in_dim.13), calls=%async_computation.9 | async-start | bytes 65536 | tf_op jit(solution)/shard_map/signal/all_to_all | solution.py:430
Sparse Core Ops, SparseCore 0:
  12.3 77.9 all-gather.4
  162.1 47.3 all-gather.6
where the time goes:
time: 310 us; the launch traced here: 309 us
  waiting for transfers between devices  127 us (41%)
  starting transfers between devices  49.3 us (16%)
  Pallas kernels  36.4 us (12%)
  local copies, waits for them, and re-layouts  33.1 us (11%)
  blocking collectives  30 us (10%)
  other arithmetic  14.7 us (5%)
  between operations  14.5 us (5%)
  matrix products  3.48 us (1%)
    all_to_all x2, waiting for transfers between devices, to_planes(): return lax.all_to_all(padded, 'col', 0, 0, tiled=True)  35.1 us
    all_to_all x1, waiting for transfers between devices, local(): received = lax.all_to_all(signal_part, 'row', 0, 0, tiled=True)  31.5 us
    unnamed x44, local copies, waits for them, and re-layouts  24.6 us
    all_to_all x1, waiting for transfers between devices, local(): lax.all_to_all(by_x, 'row', 0, 0, axis_index_groups=x_groups, tiled=True)  23.7 us
    all_to_all x1, blocking collectives, local(): lax.all_to_all(ready, 'row', 0, 0, tiled=True)  16.9 us
    all_to_all x1, waiting for transfers between devices, local(): change = lax.all_to_all(change, 'col', 0, 0, tiled=True)  16.6 us
    pallas_call x1, Pallas kernels, make_solve(): pl.pallas_call(solve_kernel, out_shape=(jax.ShapeDtypeStruct((TOTAL, TOTA...  13.9 us
    all_to_all x1, blocking collectives, local(): both = lax.all_to_all(both, 'col', 0, 0, tiled=True)  13.1 us
  transfers between devices with their start and end apart: 20, of which 15 were waited for; matrix products, arithmetic and copies ran while one was open for 7% of the time, Pallas kernels for 7%

commit v1 on v0

--- a/solution.py
+++ b/solution.py
@@ -14,7 +14,6 @@
 PANEL = 8
 WINDOW = 48
 SHARE = TOTAL // 16
-SHARE_PAD = 32
 
 loading = 1.0
 epsilon = 1e-06
@@ -23,7 +22,7 @@
 bf16 = jnp.bfloat16
 VMEM = pl.BlockSpec(memory_space=pltpu.VMEM)
 SMEM = pl.BlockSpec(memory_space=pltpu.SMEM)
-ANY = pl.BlockSpec(memory_space=pl.ANY)
+HBM = pl.BlockSpec(memory_space=pltpu.HBM)
 
 
 def params():
@@ -67,61 +66,75 @@
     return (ids == place_ref[g]).astype(f32).astype(bf16)
 
 
-def start_windows(gathered_ref, window_ref, sems, groups, per_group):
+def start_inputs(gathered_ref, channel_ref, window_ref, held_ref, sems, groups, per_group):
     copies = []
     for g in range(groups):
         start = g * per_group // 16 * 16
-        copy = pltpu.make_async_copy(
-            gathered_ref.at[:, pl.ds(start, WINDOW), :], window_ref.at[g], sems.at[g]
+        window = pltpu.make_async_copy(
+            gathered_ref.at[:, pl.ds(start, WINDOW), :], window_ref.at[g], sems.at[0, g]
         )
-        copy.start()
-        copies.append(copy)
+        channel = pltpu.make_async_copy(channel_ref.at[g], held_ref.at[g], sems.at[1, g])
+        window.start()
+        channel.start()
+        copies.append((window, channel))
     return copies
 
 
-def columns_kernel(gathered_ref, channel_ref, place_ref, few_ref, out_ref, window_ref, sems):
-    groups, user_rows, antennas = channel_ref.shape
-    copies = start_windows(gathered_ref, window_ref, sems, groups, 2 * EPOCHS * 6)
+def input_scratch(groups, user_rows, antennas):
+    return [
+        pltpu.VMEM((groups, 16, WINDOW, antennas), bf16),
+        pltpu.VMEM((groups, user_rows, antennas), bf16),
+        pltpu.SemaphoreType.DMA((2, groups)),
+    ]
+
+
+def columns_kernel(
+    row_ref, gathered_ref, channel_ref, place_ref, out_ref, window_ref, held_ref, sems
+):
+    groups, user_rows, antennas = held_ref.shape
+    copies = start_inputs(
+        gathered_ref, channel_ref, window_ref, held_ref, sems, groups, 2 * EPOCHS * 6
+    )
     out_ref[groups] = jnp.zeros(out_ref.shape[1:], bf16)
     for g in range(groups):
         choose = choosing(place_ref, g)
-        lanes = lax.broadcasted_iota(jnp.int32, (SHARE_PAD, 16 * WINDOW), 1)
-        choose_few = (lanes == few_ref[g]).astype(f32).astype(bf16)
-        copies[g].wait()
+        for copy in copies[g]:
+            copy.wait()
         window = window_ref[g].reshape(16 * WINDOW, antennas)
-        few = dot(choose_few, window).astype(bf16)
-        wide = dot_t(channel_ref[g], window).astype(bf16)
-        wide_few = dot_t(few, window).astype(bf16)
+        wide = dot_t(held_ref[g], window).astype(bf16)
         out_ref[g, :user_rows] = dot(wide, choose).astype(bf16)
-        out_ref[g, user_rows:] = dot(wide_few, choose).astype(bf16)
-
-
-def make_columns(gathered, channels, place, few):
+        wide = dot_t(window_ref[g, row_ref[0]], window).astype(bf16)
+        out_ref[g, user_rows:] = dot(wide, choose).astype(bf16)
+
+
+def make_columns(row, gathered, channels, place):
     groups, user_rows, antennas = channels.shape
     return pl.pallas_call(
         columns_kernel,
-        out_shape=jax.ShapeDtypeStruct((groups + 1, user_rows + SHARE_PAD, TOTAL), bf16),
-        in_specs=[ANY, VMEM, VMEM, VMEM],
+        out_shape=jax.ShapeDtypeStruct((groups + 1, user_rows + WINDOW, TOTAL), bf16),
+        in_specs=[SMEM, HBM, HBM, VMEM],
         out_specs=VMEM,
-        scratch_shapes=[
-            pltpu.VMEM((groups, 16, WINDOW, antennas), bf16),
-            pltpu.SemaphoreType.DMA((groups,)),
-        ],
+        scratch_shapes=input_scratch(groups, user_rows, antennas),
         compiler_params=params(),
         cost_estimate=cost(4_000_000_000, 12_000_000),
         name="columns",
-    )(gathered, channels, place, few)
-
-
-def channel_kernel(first_ref, gathered_ref, channel_ref, place_ref, slots_ref, out_ref, window_ref, sems):
-    groups, user_rows, antennas = channel_ref.shape
-    copies = start_windows(gathered_ref, window_ref, sems, groups, 2 * EPOCHS * 6)
+    )(row, gathered, channels, place)
+
+
+def channel_kernel(
+    first_ref, gathered_ref, channel_ref, place_ref, slots_ref, out_ref, window_ref, held_ref, sems
+):
+    groups, user_rows, antennas = held_ref.shape
+    copies = start_inputs(
+        gathered_ref, channel_ref, window_ref, held_ref, sems, groups, 2 * EPOCHS * 6
+    )
     for g in range(groups):
         here = placing(slots_ref.at[g], first_ref[0], user_rows).astype(bf16)
         route = dot_t(here, choosing(place_ref, g)).astype(bf16)
-        copies[g].wait()
+        for copy in copies[g]:
+            copy.wait()
         window = window_ref[g].reshape(16 * WINDOW, antennas)
-        out_ref[g] = channel_ref[g] + dot(route, window).astype(bf16)
+        out_ref[g] = held_ref[g] + dot(route, window).astype(bf16)
 
 
 def make_channel(first, gathered, channels, place, slots_mine):
@@ -129,12 +142,9 @@
     return pl.pallas_call(
         channel_kernel,
         out_shape=jax.ShapeDtypeStruct(channels.shape, bf16),
-        in_specs=[SMEM, ANY, VMEM, VMEM, VMEM],
+        in_specs=[SMEM, HBM, HBM, VMEM, VMEM],
         out_specs=VMEM,
-        scratch_shapes=[
-            pltpu.VMEM((groups, 16, WINDOW, antennas), bf16),
-            pltpu.SemaphoreType.DMA((groups,)),
-        ],
+        scratch_shapes=input_scratch(groups, user_rows, antennas),
         compiler_params=params(),
         cost_estimate=cost(4_000_000_000, 14_000_000),
         name="channel",
@@ -142,30 +152,32 @@
 
 
 def middle_kernel(
-    where_ref, square_ref, own_ref, row1_ref, row2_ref, row3_ref, col1_ref, col2_ref, col3_ref,
-    columns_ref, precoded_ref, slots_ref, first_out, block1_out, block2_out, block3_out, packed_out,
+    where_ref, square0_ref, square1_ref, square2_ref, square3_ref, own_ref, row1_ref, row2_ref,
+    row3_ref, col1_ref, col2_ref, col3_ref, columns_ref, precoded_ref, slots_ref, gram_ref,
+    place_ref, first_out, block1_out, block2_out, block3_out, packed_out,
 ):
-    y, x, first = where_ref[0], where_ref[1], where_ref[2]
+    y, row, first = where_ref[0], where_ref[1], where_ref[2]
     user_rows = own_ref.shape[0]
+    squares = [square0_ref, square1_ref, square2_ref, square3_ref]
     by_row = [own_ref, row1_ref, row2_ref, row3_ref]
     by_col = [own_ref, col1_ref, col2_ref, col3_ref]
     outs = [first_out, block1_out, block2_out, block3_out]
-    schur = None
+    ids = row * WINDOW + lax.broadcasted_iota(jnp.int32, (WINDOW, TOTAL), 0)
+    choose = (ids == place_ref[...]).astype(f32).astype(bf16)
+    schur = -t_dot(choose, gram_ref[...].astype(bf16))
     for d in range(4):
-        rows = pl.ds(pl.multiple_of((x + d) % 4 * user_rows, user_rows), user_rows)
-        block = dot(square_ref[y, rows, :], own_ref[...])
+        block = dot(squares[d][y], own_ref[...])
         for e in range(1, 4):
-            block += dot(square_ref[(y + e) % 4, rows, :], by_col[e][...])
+            block += dot(squares[d][(y + e) % 4], by_col[e][...])
         low = block.astype(bf16)
         outs[d][...] = block if d == 0 else low
-        part = t_dot(by_row[d][...], low)
-        schur = part if d == 0 else schur + part
+        schur += t_dot(by_row[d][...], low)
     packed_out[:, :TOTAL] = schur.astype(bf16)
     border = columns_ref[...] - placing(slots_ref, first, user_rows)
     packed_out[:, TOTAL:] = split(t_dot, border, precoded_ref[...]).astype(bf16)
 
 
-def make_middle(where, square, by_row, by_col, columns, precoded, slot_plane):
+def make_middle(where, squares, by_row, by_col, columns, precoded, slot_plane, gram, place_plane):
     shape = columns.shape
     return pl.pallas_call(
         middle_kernel,
@@ -176,12 +188,12 @@
             jax.ShapeDtypeStruct(shape, bf16),
             jax.ShapeDtypeStruct((TOTAL, TOTAL + STREAMS), bf16),
         ),
-        in_specs=[SMEM] + [VMEM] * 11,
+        in_specs=[SMEM] + [VMEM] * 16,
         out_specs=(VMEM,) * 5,
         compiler_params=params(),
         cost_estimate=cost(2_000_000_000, 8_000_000),
         name="middle",
-    )(where, square, *by_row, *by_col[1:], columns, precoded, slot_plane)
+    )(where, *squares, *by_row, *by_col[1:], columns, precoded, slot_plane, gram, place_plane)
 
 
 def invert_block(a):
@@ -255,51 +267,74 @@
     )(first, whole, weighted, precoded, slot_plane)
 
 
-def signal_kernel(users_ref, channel_ref, out_ref):
-    part = t_dot(users_ref[0], channel_ref[0]).astype(bf16)
-    out_ref[...] = part.reshape(out_ref.shape)
+def signal_kernel(users_ref, channel_ref, out_ref, held_ref, sems):
+    groups, _, antennas = channel_ref.shape
+    tile = antennas // 2
+    copies = []
+    for g in range(groups):
+        for m in range(0, antennas, tile):
+            part = t_dot(users_ref[g], channel_ref[g, :, m:m + tile]).astype(bf16)
+            held_ref[g, :, :, m:m + tile] = part.reshape(16, STREAMS // 16, tile)
+        copy = pltpu.make_async_copy(held_ref.at[g], out_ref.at[:, g], sems.at[g])
+        copy.start()
+        copies.append(copy)
+    for copy in copies:
+        copy.wait()
 
 
 def make_signal(users_side, channel):
-    groups, user_rows, antennas = channel.shape
-    tile = 1024
+    groups, _, antennas = channel.shape
     each = STREAMS // 16
     return pl.pallas_call(
         signal_kernel,
         out_shape=jax.ShapeDtypeStruct((16, groups, each, antennas), bf16),
-        grid=(groups, antennas // tile),
-        in_specs=[
-            pl.BlockSpec((1, user_rows, STREAMS), lambda g, m: (g, 0, 0)),
-            pl.BlockSpec((1, user_rows, tile), lambda g, m: (g, 0, m)),
+        in_specs=[VMEM, VMEM],
+        out_specs=HBM,
+        scratch_shapes=[
+            pltpu.VMEM((groups, 16, each, antennas), bf16),
+            pltpu.SemaphoreType.DMA((groups,)),
         ],
-        out_specs=pl.BlockSpec((16, 1, each, tile), lambda g, m: (0, g, 0, m)),
         compiler_params=params(),
         cost_estimate=cost(800_000_000, 7_000_000),
         name="signal",
     )(users_side, channel)
 
 
-def update_kernel(first_ref, weighted_ref, inv_ref, all_ref, slots_ref, out_ref):
+def update_kernel(
+    where_ref, weighted_ref, inv_ref, all_ref, slots_ref, out0, out1, out2, out3, held_ref, sems
+):
+    first, plane = where_ref[0], where_ref[1]
     user_rows = weighted_ref.shape[0]
-    border = weighted_ref[...] - placing(slots_ref, first_ref[0], user_rows)
+    border = weighted_ref[...] - placing(slots_ref, first, user_rows)
     half = split(dot, border, inv_ref[...]).astype(bf16)
-    for z in range(4):
-        there = all_ref[4 * z:4 * z + 4].reshape(4 * user_rows, TOTAL).astype(f32)
+    copies = []
+    for d, out in enumerate([out0, out1, out2, out3]):
+        z = (plane + d) % 4
+        there = all_ref[pl.ds(4 * z, 4)].reshape(4 * user_rows, TOTAL).astype(f32)
         there = there - placing(slots_ref, 4 * user_rows * z, 4 * user_rows)
-        out_ref[z] = dot_t(half, there.astype(bf16)).astype(bf16)
-
-
-def make_update(first, weighted, schur_inverse, weighted_all, slot_plane):
+        held_ref[d] = dot_t(half, there.astype(bf16)).astype(bf16)
+        copy = pltpu.make_async_copy(held_ref.at[d], out, sems.at[d])
+        copy.start()
+        copies.append(copy)
+    for copy in copies:
+        copy.wait()
+
+
+def make_update(where, weighted, schur_inverse, weighted_all, slot_plane):
     user_rows = weighted.shape[0]
     return pl.pallas_call(
         update_kernel,
-        out_shape=jax.ShapeDtypeStruct((4, user_rows, 4 * user_rows), bf16),
+        out_shape=(jax.ShapeDtypeStruct((user_rows, 4 * user_rows), bf16),) * 4,
         in_specs=[SMEM] + [VMEM] * 4,
-        out_specs=VMEM,
+        out_specs=(HBM,) * 4,
+        scratch_shapes=[
+            pltpu.VMEM((4, user_rows, 4 * user_rows), bf16),
+            pltpu.SemaphoreType.DMA((4,)),
+        ],
         compiler_params=params(),
         cost_estimate=cost(1_500_000_000, 8_000_000),
         name="update",
-    )(first, weighted, schur_inverse, weighted_all, slot_plane)
+    )(where, weighted, schur_inverse, weighted_all, slot_plane)
 
 
 def local(channels, inverse, arrivals, arrival_cell, cell_owner, slots, symbols):
@@ -311,7 +346,6 @@
     row_index = lax.axis_index("row")
     col_index = lax.axis_index("col")
     y_index, x_index = row_index // 4, row_index % 4
-    x_groups = [[4 * y + x for x in range(4)] for y in range(4)]
 
     def along_x(value, step):
         pairs = [(4 * y + x, 4 * y + (x + step) % 4) for y in range(4) for x in range(4)]
@@ -320,6 +354,9 @@
     def along_y(value, step):
         pairs = [(4 * y + x, 4 * ((y + step) % 4) + x) for y in range(4) for x in range(4)]
         return lax.ppermute(value, "row", pairs)
+
+    def along_z(value, step):
+        return lax.ppermute(value, "col", [(z, (z + step) % 4) for z in range(4)])
 
     def to_planes(value):
         padded = jnp.concatenate([value, jnp.zeros_like(value[:1])], axis=0)
@@ -344,10 +381,7 @@
 
     with jax.named_scope("planes"):
         low = inverse.astype(bf16).reshape(group_count, user_rows, 4, user_rows)
-        by_x = low.transpose(2, 0, 1, 3)
-        by_x = lax.all_to_all(by_x, "row", 0, 0, axis_index_groups=x_groups, tiled=True)
-        by_group = by_x.transpose(1, 0, 2, 3).reshape(group_count, 4 * user_rows, user_rows)
-        square = to_planes(by_group)
+        full_rows = to_planes(low.transpose(0, 2, 1, 3))
         symbol_part = jnp.einsum(
             "grc,gcs->grs", inverse, symbols.astype(f32), precision=highest
         )
@@ -375,37 +409,46 @@
         inside = offset[:, None] + epoch[None, :] * 2 * capacity
         inside = inside[:, :, None] + owners // 16 * capacity + ranking
         place = (owners % 16 * WINDOW + inside).reshape(group_count, 1, TOTAL)
-        few = lax.dynamic_slice_in_dim(place, row_index * SHARE, SHARE, 2)
-        few = jnp.pad(few, ((0, 0), (0, 0), (0, SHARE_PAD - SHARE)), constant_values=-1)
-        few = few.reshape(group_count, SHARE_PAD, 1)
+        plane_place = lax.dynamic_slice_in_dim(
+            place, jnp.minimum(col_index, group_count - 1), 1, 0
+        ).reshape(1, TOTAL)
 
     with jax.named_scope("columns"):
-        gathered, square, precoded = lax.optimization_barrier((gathered, square, precoded))
-        both = make_columns(gathered, channels, place, few)
+        gathered, full_rows, precoded = lax.optimization_barrier(
+            (gathered, full_rows, precoded)
+        )
+        squares = []
+        for d in range(4):
+            piece = lax.dynamic_index_in_dim(full_rows, (x_index + d) % 4, 1, keepdims=False)
+            squares.append(along_x(piece, d) if d else piece)
+        both = make_columns(row_index.reshape(1), gathered, channels, place)
         both = lax.all_to_all(both, "col", 0, 0, tiled=True)
         summed = jnp.sum(both.astype(f32), axis=0)
         columns = summed[:user_rows]
-        gram = summed[user_rows:user_rows + SHARE]
+        gram = summed[user_rows:]
         own = columns.astype(bf16)
-        by_row = [own] + [along_x(own, -d) for d in (1, 2, 3)]
+        by_row = [own] + [along_x(own, d) for d in (1, 2, 3)]
         by_col = [own] + [along_y(own, -d) for d in (1, 2, 3)]
 
     with jax.named_scope("schur"):
-        where = jnp.stack([y_index, x_index, first_row])
+        where = jnp.stack([y_index, row_index, first_row])
         block0, block1, block2, block3, packed = make_middle(
-            where, square, by_row, by_col, columns, precoded, slot_plane
+            where, squares, by_row, by_col, columns, precoded, slot_plane, gram, plane_place
+        )
+        packed = packed.reshape(16, SHARE, TOTAL + STREAMS)
+        shared = lax.all_to_all(packed, "row", 0, 0, tiled=True)
+        shared, block1, block2, block3 = lax.optimization_barrier(
+            (shared, block1, block2, block3)
         )
         weighted = block0
         for d, block in ((1, block1), (2, block2), (3, block3)):
-            weighted = weighted + along_x(block, d).astype(f32)
-        packed = packed.reshape(16, SHARE, TOTAL + STREAMS)
-        shared = lax.all_to_all(packed, "row", 0, 0, tiled=True).astype(f32)
-        shared = jnp.sum(shared, axis=0)
+            weighted = weighted + along_x(block, -d).astype(f32)
+        shared = jnp.sum(shared.astype(f32), axis=0)
         share_ids = row_index * SHARE + jnp.arange(SHARE, dtype=jnp.int32)
         identity = loading * (
             share_ids[:, None] == jnp.arange(TOTAL, dtype=jnp.int32)[None, :]
         ).astype(f32)
-        schur_rows = gram + identity - shared[:, :TOTAL]
+        schur_rows = identity - shared[:, :TOTAL]
         ready = jnp.concatenate([schur_rows, shared[:, TOTAL:]], axis=1)
         ready = jnp.broadcast_to(ready[None], (16, SHARE, TOTAL + STREAMS))
         whole = lax.all_to_all(ready, "row", 0, 0, tiled=True).reshape(TOTAL, TOTAL + STREAMS)
@@ -413,17 +456,20 @@
     with jax.named_scope("users"):
         weighted_all = lax.all_gather(weighted.astype(bf16), "row")
         channel = make_channel(first_arg, gathered, channels, place, slots_mine)
+        whole, channel = lax.optimization_barrier((whole, channel))
         schur_inverse, users = make_solve(first_arg, whole, weighted, precoded, slot_plane)
         users_side = lax.all_to_all(users, "col", 0, 0, tiled=True)
 
     with jax.named_scope("update"):
-        change = make_update(first_arg, weighted, schur_inverse, weighted_all, slot_plane)
-        change = lax.all_to_all(change, "col", 0, 0, tiled=True)
+        changes = make_update(
+            jnp.stack([first_row, col_index]), weighted, schur_inverse, weighted_all, slot_plane
+        )
+        changes = [changes[0]] + [along_z(changes[d], d) for d in (1, 2, 3)]
 
     with jax.named_scope("signal"):
         signal_part = make_signal(users_side, channel)
         received = lax.all_to_all(signal_part, "row", 0, 0, tiled=True)
-        received, change = lax.optimization_barrier((received, change))
+        received, changes = lax.optimization_barrier((received, changes))
         signal = jnp.sum(received.astype(f32), axis=0)
         power = jnp.sum(signal * signal, axis=(1, 2))
         power = jnp.broadcast_to(power[None, None, :], (64, 1, group_count))
@@ -437,7 +483,14 @@
         diagonal = row_ids[:, None] == col_ids[None, :]
         full = jnp.any(slots_mine == row_ids[None, :, None], axis=2)
         gone = jnp.where(diagonal[None] & full[:, :, None], 1.0 / loading, 0.0)
-        updated = inverse - gone + change[:group_count].astype(f32)
+        updated = []
+        for g in range(group_count):
+            step = (col_index - g) % 4
+            add = changes[0]
+            for d in (1, 2, 3):
+                add = jnp.where(step == d, changes[d], add)
+            updated.append(inverse[g] - gone[g] + add.astype(f32))
+        updated = jnp.stack(updated, axis=0)
     return (updated, transmit)
 
 

time: 310 us -> 298 us (0.961)
  waiting for transfers between devices: 127 us -> 116 us
  local copies, waits for them, and re-layouts: 33.1 us -> 28.2 us
    all_to_all x4 -> x2, waiting for transfers between devices: 43.8 us -> 15 us  [the longest x1 7.8 us: local(): lax.all_to_all(ready, 'row', 0, 0, tiled=True)]
    all_gather x1, waiting for transfers between devices: 0.01 us -> 13.5 us  [local(): gathered = lax.all_gather(chunk, 'row')]
    ppermute x6 -> x9, waiting for transfers between devices: 5.96 us -> 16.8 us  [along_x(): return lax.ppermute(value, 'row', pairs)]
    all_to_all x4 -> x2, starting transfers between devices: 16.4 us -> 8.97 us  [the longest x1 4.54 us: local(): lax.all_to_all(ready, 'row', 0, 0, tiled=True)]
    ppermute x6 -> x9, starting transfers between devices: 7.64 us -> 14.1 us  [along_x(): return lax.ppermute(value, 'row', pairs)]
    unnamed x44 -> x47, local copies, waits for them, and re-layouts: 24.6 us -> 18.6 us
    another operation x1 -> x4, other arithmetic: 0.08 us -> 5.54 us  [the longest x2 5.39 us: local(): updated = jnp.stack(updated, axis=0)]
    all_to_all x1, waiting for transfers between devices: 31.5 us -> 26.8 us  [local(): received = lax.all_to_all(signal_part, 'row', 0, 0, tiled=True)]
  transfers between devices with their start and end apart: 20 -> 24, of which waited for: 15 -> 14; matrix products, arithmetic and copies ran while one was open for 7% -> 9% of each run, Pallas kernels for 7% -> 9%
where the time goes in v1:
time: 298 us; the launch traced here: 297 us
  waiting for transfers between devices  116 us (39%)
  starting transfers between devices  51.5 us (17%)
  Pallas kernels  38.9 us (13%)
  local copies, waits for them, and re-layouts  28.2 us (9%)
  blocking collectives  27.2 us (9%)
  other arithmetic  16.9 us (6%)
  between operations  14.6 us (5%)
  matrix products  3.49 us (1%)
    all_to_all x2, waiting for transfers between devices, to_planes(): return lax.all_to_all(padded, 'col', 0, 0, tiled=True)  34.2 us
    all_to_all x1, waiting for transfers between devices, local(): received = lax.all_to_all(signal_part, 'row', 0, 0, tiled=True)  26.8 us
    unnamed x47, local copies, waits for them, and re-layouts  18.6 us
    ppermute x9, waiting for transfers between devices, along_x(): return lax.ppermute(value, 'row', pairs)  16.8 us
    pallas_call x1, Pallas kernels, make_solve(): pl.pallas_call(solve_kernel, out_shape=(jax.ShapeDtypeStruct((TOTAL, TOTA...  15.1 us
    all_to_all x1, blocking collectives, local(): shared = lax.all_to_all(packed, 'row', 0, 0, tiled=True)  14.8 us
    ppermute x9, starting transfers between devices, along_x(): return lax.ppermute(value, 'row', pairs)  14.1 us
    all_gather x1, waiting for transfers between devices, local(): gathered = lax.all_gather(chunk, 'row')  13.5 us
  transfers between devices with their start and end apart: 24, of which 14 were waited for; matrix products, arithmetic and copies ran while one was open for 9% of the time, Pallas kernels for 9%

profile of v1, /device:TPU:0, one launch (start us, length us, event | category | flops | bytes accessed | tf_op | source)
XLA Modules:
  0.0 296.5 jit_solution(16353080385034725504)
XLA Ops:
  7.2 1.1 constant_dynamic-slice_fusion.3
  8.4 1.6 collective-permute-done
  10.0 1.0 select_bitcast_fusion.1
  12.2 3.5 %fusion.15 = f32[3,256,256]{2,1,0:T(8,128)S(1)} fusion(f32[3,256,1024]{2,1,0:T(8,128)} %param.8, bf16[3,1024,256]{2,1,0:T(8,128)(2,1)S(1)} %copy-done), kind=kOutput, calls=%fused_computation.67 | convolution fusion | flops 2415919104 | bytes 5505024 | tf_op jit(solution)/shard_map/planes/grc,gcs->grs/dot_general | solution.py:385
  15.7 1.1 concatenate.10
  16.8 5.5 %all-to-all-start.1 = ((f32[4,256,256]{2,1,0:T(8,128)}), f32[4,256,256]{2,1,0:T(8,128)}, u32[]{:S(2)}, u32[]{:S(2)}) async-start(f32[4,256,256]{2,1,0:T(8,128)} %concatenate.10), calls=%async_computation.1 | async-start | bytes 2097152 | tf_op jit(solution)/shard_map/planes/all_to_all | solution.py:363
  22.3 1.7 copy.24
  24.0 1.8 copy.29
  25.8 1.5 concatenate.9.clone
  27.3 10.5 %all-to-all-done.1 = f32[4,256,256]{2,1,0:T(8,128)} async-done(((f32[4,256,256]{2,1,0:T(8,128)}), f32[4,256,256]{2,1,0:T(8,128)}, u32[]{:S(2)}, u32[]{:S(2)}) %all-to-all-start.1) | async-done | bytes 1048608 | tf_op jit(solution)/shard_map/planes/all_to_all | solution.py:363
  37.8 3.6 %all-to-all-start = ((bf16[4,4,256,256]{3,2,1,0:T(8,128)(2,1)}), bf16[4,4,256,256]{3,2,1,0:T(8,128)(2,1)S(1)}, u32[]{:S(2)}, u32[]{:S(2)}) async-start(bf16[4,4,256,256]{3,2,1,0:T(8,128)(2,1)} %concatenate.9.clone), calls=%async_computation | async-start | bytes 4194304 | tf_op jit(solution)/shard_map/planes/all_to_all | solution.py:363
  42.1 1.3 reduce_sum.76.precoded_ref
  43.5 23.7 %all-to-all-done = bf16[4,4,256,256]{3,2,1,0:T(8,128)(2,1)S(1)} async-done(((bf16[4,4,256,256]{3,2,1,0:T(8,128)(2,1)}), bf16[4,4,256,256]{3,2,1,0:T(8,128)(2,1)S(1)}, u32[]{:S(2)}, u32[]{:S(2)}) %all-to-all-start) | async-done | bytes 2097184 | tf_op jit(solution)/shard_map/planes/all_to_all | solution.py:363
  67.2 13.5 %all-gather.5.cloned.1.call-done = bf16[1792,2048]{1,0:T(8,128)(2,1)} async-done(((bf16[112,2048]{1,0:T(8,128)(2,1)}), bf16[1792,2048]{1,0:T(8,128)(2,1)}) %all-gather.5.cloned.1.call-update) | async-done | bytes 7340048 | tf_op jit(solution)/shard_map/newcomers/all_gather | solution.py:380
  80.7 3.1 %copy-done.7 = bf16[1792,2048]{1,0:T(8,128)(2,1)S(1)} copy-done((bf16[1792,2048]{1,0:T(8,128)(2,1)S(1)}, bf16[1792,2048]{1,0:T(8,128)(2,1)}, u32[]{:S(2)}) %copy-start.7) | copy-done | bytes 7340056
  83.8 1.9 copy-done.9
  85.6 10.7 %columns.1 = bf16[4,304,384]{2,1,0:T(8,128)(2,1)} custom-call(s32[1]{0:T(128)} %bitcast.3.row_ref, bf16[16,112,2048]{2,1,0:T(8,128)(2,1)S(1)} %bitcast.70, bf16[3,256,2048]{2,1,0:T(8,128)(2,1)S(1)} %copy-done.9, s32[3,1,384]{2,1,0:T(1,128)S(1)} %fusion.10.place_ref), custom_call_target="tpu_custom_call" | custom-call | flops 4000000000 | bytes 12000000 | tf_op jit(solution)/shard_map/columns/columns/pallas_call | solution.py:112
  96.4 4.4 %all-to-all-start.2 = ((bf16[4,304,384]{2,1,0:T(8,128)(2,1)}), bf16[4,304,384]{2,1,0:T(8,128)(2,1)}, u32[]{:S(2)}, u32[]{:S(2)}) async-start(bf16[4,304,384]{2,1,0:T(8,128)(2,1)} %columns.1), calls=%async_computation.2 | async-start | bytes 1867776 | tf_op jit(solution)/shard_map/columns/all_to_all | solution.py:425
  100.8 1.2 dynamic-slice_bitcast_fusion
  102.0 1.5 collective-permute-start.1
  103.5 2.7 collective-permute-start.2
  106.2 1.5 collective-permute-start.3
  107.6 7.2 %all-to-all-done.2 = bf16[4,304,384]{2,1,0:T(8,128)(2,1)} async-done(((bf16[4,304,384]{2,1,0:T(8,128)(2,1)}), bf16[4,304,384]{2,1,0:T(8,128)(2,1)}, u32[]{:S(2)}, u32[]{:S(2)}) %all-to-all-start.2) | async-done | bytes 933920 | tf_op jit(solution)/shard_map/columns/all_to_all | solution.py:425
  114.8 1.4 convert_reduce_fusion.1
  117.0 1.7 collective-permute-start.4
  119.4 2.7 collective-permute-start.5
  122.1 1.4 collective-permute-start.6
  123.5 7.0 %collective-permute-done.2.square2_ref = bf16[4,256,256]{2,1,0:T(8,128)(2,1)S(1)} collective-permute-done((bf16[4,256,256]{2,1,0:T(8,128)(2,1)}, bf16[4,256,256]{2,1,0:T(8,128)(2,1)S(1)}, u32[]{:S(2)}, u32[]{:S(2)}) %collective-permute-start.2) | collective-permute-done | bytes 524320 | tf_op jit(solution)/shard_map/columns/ppermute | solution.py:352
  130.5 1.3 collective-permute-start.7
  131.8 1.6 collective-permute-start.8
  133.4 1.2 collective-permute-done.4.row1_ref
  134.6 3.6 %collective-permute-start.9 = (bf16[256,384]{1,0:T(8,128)(2,1)S(1)}, bf16[256,384]{1,0:T(8,128)(2,1)S(1)}, u32[]{:S(2)}, u32[]{:S(2)}) collective-permute-start(bf16[256,384]{1,0:T(8,128)(2,1)S(1)} %slice.73.own_ref), channel_id=1, source_target_pairs={{0,16},{4,20},{8,24},{12,28},{16,32},{20,36},{24,40},{28,44},{32,4... | collective-permute-start | bytes 589832 | tf_op jit(solution)/shard_map/columns/ppermute | solution.py:356
  138.2 1.0 slice.41.columns_ref
  139.3 0.9 slice.42.gram_ref
  140.2 3.7 %collective-permute-done.9.col3_ref = bf16[256,384]{1,0:T(8,128)(2,1)S(1)} collective-permute-done((bf16[256,384]{1,0:T(8,128)(2,1)S(1)}, bf16[256,384]{1,0:T(8,128)(2,1)S(1)}, u32[]{:S(2)}, u32[]{:S(2)}) %collective-permute-start.9) | collective-permute-done | bytes 196640 | tf_op jit(solution)/shard_map/columns/ppermute | solution.py:356
  143.8 2.9 middle.1
  146.7 14.8 %all_to_all.40 = bf16[16,24,640]{2,1,0:T(8,128)(2,1)S(1)} all-to-all(bf16[16,24,640]{2,1,0:T(8,128)(2,1)S(1)} %bitcast.66), channel_id=1, replica_groups=mesh['grp'=2,'row'=16,'col'=4] {'row'}, dimensions={0} | all-to-all | bytes 983040 | tf_op jit(solution)/shard_map/schur/all_to_all | solution.py:439
  162.0 2.2 collective-permute-start.11
  164.2 4.3 %collective-permute-done.10 = bf16[256,384]{1,0:T(8,128)(2,1)S(1)} collective-permute-done((bf16[256,384]{1,0:T(8,128)(2,1)S(1)}, bf16[256,384]{1,0:T(8,128)(2,1)S(1)}, u32[]{:S(2)}, u32[]{:S(2)}) %collective-permute-start.10) | collective-permute-done | bytes 196640 | tf_op jit(solution)/shard_map/schur/ppermute | solution.py:352
  168.5 2.3 collective-permute-done.11
  170.7 2.0 collective-permute-done.12
  173.8 1.0 broadcast_in_dim.12
  174.8 4.5 %all-to-all-start.4 = ((f32[16,24,640]{2,1,0:T(8,128)}), f32[16,24,640]{2,1,0:T(8,128)}, u32[]{:S(2)}, u32[]{:S(2)}) async-start(f32[16,24,640]{2,1,0:T(8,128)} %broadcast_in_dim.12), calls=%async_computation.4 | async-start | bytes 1966080 | tf_op jit(solution)/shard_map/schur/all_to_all | solution.py:454
  179.4 3.2 %copy-done.8 = bf16[1792,2048]{1,0:T(8,128)(2,1)S(1)} copy-done((bf16[1792,2048]{1,0:T(8,128)(2,1)S(1)}, bf16[1792,2048]{1,0:T(8,128)(2,1)}, u32[]{:S(2)}) %copy-start.8) | copy-done | bytes 7340056
  182.6 1.9 copy-done.10
  184.5 4.8 %channel.1.channel_ref = bf16[3,256,2048]{2,1,0:T(8,128)(2,1)S(1)} custom-call(s32[1]{0:T(128)} %bitcast.1.first_ref, bf16[16,112,2048]{2,1,0:T(8,128)(2,1)S(1)} %bitcast.71, bf16[3,256,2048]{2,1,0:T(8,128)(2,1)S(1)} %copy-done.10, s32[3,1,384]{2,1,0:T(1,128)S(1)} %fusion.10.place_ref, s32[3,1,384]{2,1,0:T(1,128)S(1)} %reshape.281.slots_ref), custom_call_target="tpu_custom_call" | custom-call | flops 4000000000 | bytes 14000000 | tf_op jit(solution)/shard_map/users/channel/pallas_call | solution.py:142
  189.3 7.8 %all-to-all-done.4 = f32[16,24,640]{2,1,0:T(8,128)} async-done(((f32[16,24,640]{2,1,0:T(8,128)}), f32[16,24,640]{2,1,0:T(8,128)}, u32[]{:S(2)}, u32[]{:S(2)}) %all-to-all-start.4) | async-done | bytes 983072 | tf_op jit(solution)/shard_map/schur/all_to_all | solution.py:454
  197.1 0.9 copy-done.3
  198.7 15.1 %solve.1 = (f32[384,384]{1,0:T(8,128)S(1)}, bf16[4,256,256]{2,1,0:T(8,128)(2,1)S(1)}) custom-call(s32[1]{0:T(128)} %bitcast.1.first_ref, f32[384,640]{1,0:T(8,128)} %bitcast.15.whole_ref, f32[256,384]{1,0:T(8,128)S(1)} %get-tuple-element.53.weighted_ref, f32[256,256]{1,0:T(8,128)S(1)} %copy-done.3, s32[1,384]{1,0:T(1,128)S(1)} %bitcast.68), custom_call_target="tpu_custom_call" | custom-call | flops 10000000000 | bytes 4000000 | tf_op jit(solution)/shard_map/users/solve/pallas_call | solution.py:256
  213.9 12.4 %all_to_all.41.users_ref = bf16[4,256,256]{2,1,0:T(8,128)(2,1)S(1)} all-to-all(bf16[4,256,256]{2,1,0:T(8,128)(2,1)S(1)} %get-tuple-element.40), channel_id=1, replica_groups=mesh['grp'=2,'row'=16,'col'=4] {'col'}, dimensions={0} | all-to-all | bytes 1048576 | tf_op jit(solution)/shard_map/users/all_to_all | solution.py:461
  226.3 2.2 signal.1
  228.5 4.6 %all-to-all-start.6 = ((bf16[16,3,16,2048]{3,2,1,0:T(8,128)(2,1)}), bf16[16,3,16,2048]{3,2,1,0:T(8,128)(2,1)}, u32[]{:S(2)}, u32[]{:S(2)}) async-start(bf16[16,3,16,2048]{3,2,1,0:T(8,128)(2,1)} %signal.1), calls=%async_computation.6 | async-start | bytes 6291456 | tf_op jit(solution)/shard_map/signal/all_to_all | solution.py:471
  233.6 1.9 copy-done.11
  235.5 3.2 %update.1 = (bf16[256,1024]{1,0:T(8,128)(2,1)S(1)}, bf16[256,1024]{1,0:T(8,128)(2,1)S(1)}, bf16[256,1024]{1,0:T(8,128)(2,1)S(1)}, bf16[256,1024]{1,0:T(8,128)(2,1)S(1)}) custom-call(s32[2]{0:T(128)S(1)} %pad_add_fusion.1.where_ref, f32[256,384]{1,0:T(8,128)S(1)} %get-tuple-element.53.weighted_ref, f32[384,384]{1,0:T(8,128)S(1)} %copy-done.13, ...), custom_call_target="tpu_custom_call" | custom-call | flops 1500000000 | bytes 8000000 | tf_op jit(solution)/shard_map/update/update/pallas_call | solution.py:325
  239.4 2.1 collective-permute-start.14
  241.5 0.8 collective-permute-start.15
  242.5 2.1 and_select_fusion
  244.6 26.8 %all-to-all-done.6 = bf16[16,3,16,2048]{3,2,1,0:T(8,128)(2,1)} async-done(((bf16[16,3,16,2048]{3,2,1,0:T(8,128)(2,1)}), bf16[16,3,16,2048]{3,2,1,0:T(8,128)(2,1)}, u32[]{:S(2)}, u32[]{:S(2)}) %all-to-all-start.6) | async-done | bytes 3145760 | tf_op jit(solution)/shard_map/signal/all_to_all | solution.py:471
  271.4 2.5 convert_reduce_fusion
  274.7 4.6 %all-to-all-start.7 = ((f32[64,1,3]{2,1,0:T(1,128)}), f32[64,1,3]{2,1,0:T(1,128)S(1)}, u32[]{:S(2)}, u32[]{:S(2)}) async-start(f32[64,1,3]{2,1,0:T(1,128)} %broadcast_in_dim.13), calls=%async_computation.7 | async-start | bytes 65536 | tf_op jit(solution)/shard_map/signal/all_to_all | solution.py:476
  279.3 3.5 %fusion.8 = (f32[1,256,1024]{2,1,0:T(8,128)S(1)}, f32[1,256,1024]{2,1,0:T(8,128)S(1)}, f32[1,256,1024]{2,1,0:T(8,128)S(1)}) fusion(f32[3,256,1024]{2,1,0:T(8,128)} %and_select_fusion, f32[3,256,1024]{2,1,0:T(8,128)} %param.8, bf16[256,1024]{1,0:T(8,128)(2,1)} %collective-permute-done.15, bf16[256,1024]{1,0:T(8,128)(2,1)S(1)} %collective-permute-done.14, ...), kind=kLoop, calls=%fused_computation.16 | loop fusion | flops 4718592 | bytes 11534345 | tf_op jit(solution)/shard_map/final/stack | solution.py:493
  282.8 1.9 pad_maximum_fusion
  284.7 4.1 %all-to-all-done.7 = f32[64,1,3]{2,1,0:T(1,128)S(1)} async-done(((f32[64,1,3]{2,1,0:T(1,128)}), f32[64,1,3]{2,1,0:T(1,128)S(1)}, u32[]{:S(2)}, u32[]{:S(2)}) %all-to-all-start.7) | async-done | bytes 800 | tf_op jit(solution)/shard_map/signal/all_to_all | solution.py:476
  288.8 0.8 multiply_bitcast_fusion
  (92 shorter events, 7.8 us)
Async XLA Ops:
  7.2 5.0 %copy-start = (bf16[3,1024,256]{2,1,0:T(8,128)(2,1)S(1)}, bf16[3,1024,256]{2,1,0:T(8,128)(2,1)}, u32[]{:S(2)}) copy-start(bf16[3,1024,256]{2,1,0:T(8,128)(2,1)} %param.13) | copy-start | bytes 4718596
  7.2 73.5 %all-gather.5.cloned.1.call-start = ((), (), s32[]{:S(2)}) async-start(), calls=%async_computation.8 | async-start | bytes 7798784 | tf_op jit(solution)/shard_map/newcomers/all_gather | solution.py:380
  8.3 1.7 collective-permute-start
  15.7 6.6 %copy-start.14 = (f32[3,256,1024]{2,1,0:T(8,128)S(1)}, f32[3,256,1024]{2,1,0:T(8,128)}, u32[]{:S(2)}) copy-start(f32[3,256,1024]{2,1,0:T(8,128)} %param.8) | copy-start | bytes 9437188
  16.8 21.0 %all-to-all-start.1 = ((f32[4,256,256]{2,1,0:T(8,128)}), f32[4,256,256]{2,1,0:T(8,128)}, u32[]{:S(2)}, u32[]{:S(2)}) async-start(f32[4,256,256]{2,1,0:T(8,128)} %concatenate.10), calls=%async_computation.1 | async-start | bytes 2097152 | tf_op jit(solution)/shard_map/planes/all_to_all | solution.py:363
  25.8 15.7 %copy-start.18 = (s32[6,3,128,1]{2,3,1,0:T(1,128)S(1)}, s32[6,3,128,1]{2,3,1,0:T(1,128)}, u32[]{:S(2)}) copy-start(s32[6,3,128,1]{2,3,1,0:T(1,128)} %param.10) | copy-start | bytes 27652
  25.8 16.0 %copy-start.19 = (s32[32]{0:T(128)S(1)}, s32[32]{0:T(128)}, u32[]{:S(2)}) copy-start(s32[32]{0:T(128)} %param.11) | copy-start | bytes 388
  37.8 29.3 %all-to-all-start = ((bf16[4,4,256,256]{3,2,1,0:T(8,128)(2,1)}), bf16[4,4,256,256]{3,2,1,0:T(8,128)(2,1)S(1)}, u32[]{:S(2)}, u32[]{:S(2)}) async-start(bf16[4,4,256,256]{3,2,1,0:T(8,128)(2,1)} %concatenate.9.clone), calls=%async_computation | async-start | bytes 4194304 | tf_op jit(solution)/shard_map/planes/all_to_all | solution.py:363
  43.5 100.4 %copy-start.2 = (f32[256,256]{1,0:T(8,128)}, f32[256,256]{1,0:T(8,128)S(1)}, u32[]{:S(2)}) copy-start(f32[256,256]{1,0:T(8,128)S(1)} %reduce_sum.76.precoded_ref) | copy-start | bytes 786436
  80.7 3.1 %copy-start.7 = (bf16[1792,2048]{1,0:T(8,128)(2,1)S(1)}, bf16[1792,2048]{1,0:T(8,128)(2,1)}, u32[]{:S(2)}) copy-start(bf16[1792,2048]{1,0:T(8,128)(2,1)} %all-gather.5.cloned.1.call-done) | copy-start | bytes 22020100
  83.8 1.9 copy-start.9
  96.4 18.4 %all-to-all-start.2 = ((bf16[4,304,384]{2,1,0:T(8,128)(2,1)}), bf16[4,304,384]{2,1,0:T(8,128)(2,1)}, u32[]{:S(2)}, u32[]{:S(2)}) async-start(bf16[4,304,384]{2,1,0:T(8,128)(2,1)} %columns.1), calls=%async_computation.2 | async-start | bytes 1867776 | tf_op jit(solution)/shard_map/columns/all_to_all | solution.py:425
  100.8 132.8 %all-gather.7.cloned.1.call-start = ((), (), s32[]{:S(2)}) async-start(), calls=%async_computation.9 | async-start | bytes 3342336 | tf_op jit(solution)/shard_map/users/all_gather | solution.py:457
  102.0 20.0 %collective-permute-start.1 = (bf16[4,256,256]{2,1,0:T(8,128)(2,1)}, bf16[4,256,256]{2,1,0:T(8,128)(2,1)S(1)}, u32[]{:S(2)}, u32[]{:S(2)}) collective-permute-start(bf16[4,256,256]{2,1,0:T(8,128)(2,1)} %get-tuple-element.59), channel_id=1, source_target_pairs={{0,4},{4,8},{8,12},{12,0},{16,20},{20,24},{24,28},{28,16},{32,36},... | collective-permute-start | bytes 1572872 | tf_op jit(solution)/shard_map/columns/ppermute | solution.py:352
  103.5 27.0 %collective-permute-start.2 = (bf16[4,256,256]{2,1,0:T(8,128)(2,1)}, bf16[4,256,256]{2,1,0:T(8,128)(2,1)S(1)}, u32[]{:S(2)}, u32[]{:S(2)}) collective-permute-start(bf16[4,256,256]{2,1,0:T(8,128)(2,1)} %get-tuple-element.58), channel_id=1, source_target_pairs={{0,8},{4,12},{8,0},{12,4},{16,24},{20,28},{24,16},{28,20},{32,40},... | collective-permute-start | bytes 1572872 | tf_op jit(solution)/shard_map/columns/ppermute | solution.py:352
  106.2 25.6 %collective-permute-start.3 = (bf16[4,256,256]{2,1,0:T(8,128)(2,1)}, bf16[4,256,256]{2,1,0:T(8,128)(2,1)S(1)}, u32[]{:S(2)}, u32[]{:S(2)}) collective-permute-start(bf16[4,256,256]{2,1,0:T(8,128)(2,1)} %get-tuple-element.57), channel_id=1, source_target_pairs={{0,12},{4,0},{8,4},{12,8},{16,28},{20,16},{24,20},{28,24},{32,44},... | collective-permute-start | bytes 1572872 | tf_op jit(solution)/shard_map/columns/ppermute | solution.py:352
  116.2 0.8 copy-start.15
  117.0 17.6 %collective-permute-start.4 = (bf16[256,384]{1,0:T(8,128)(2,1)S(1)}, bf16[256,384]{1,0:T(8,128)(2,1)S(1)}, u32[]{:S(2)}, u32[]{:S(2)}) collective-permute-start(bf16[256,384]{1,0:T(8,128)(2,1)S(1)} %slice.73.own_ref), channel_id=1, source_target_pairs={{0,4},{4,8},{8,12},{12,0},{16,20},{20,24},{24,28},{28,16},{32,36},... | collective-permute-start | bytes 589832 | tf_op jit(solution)/shard_map/columns/ppermute | solution.py:352
  119.4 27.3 %copy-start.4 = (s32[1,1,3,128]{3,1,2,0:T(1,128)}, s32[1,1,3,128]{3,1,2,0:T(1,128)S(1)}, u32[]{:S(2)}) copy-start(s32[1,1,3,128]{3,1,2,0:T(1,128)S(1)} %copy.37) | copy-start | bytes 4612
  119.4 20.8 %collective-permute-start.5 = (bf16[256,384]{1,0:T(8,128)(2,1)S(1)}, bf16[256,384]{1,0:T(8,128)(2,1)S(1)}, u32[]{:S(2)}, u32[]{:S(2)}) collective-permute-start(bf16[256,384]{1,0:T(8,128)(2,1)S(1)} %slice.73.own_ref), channel_id=1, source_target_pairs={{0,8},{4,12},{8,0},{12,4},{16,24},{20,28},{24,16},{28,20},{32,40},... | collective-permute-start | bytes 589832 | tf_op jit(solution)/shard_map/columns/ppermute | solution.py:352
  122.1 18.1 %collective-permute-start.6 = (bf16[256,384]{1,0:T(8,128)(2,1)S(1)}, bf16[256,384]{1,0:T(8,128)(2,1)S(1)}, u32[]{:S(2)}, u32[]{:S(2)}) collective-permute-start(bf16[256,384]{1,0:T(8,128)(2,1)S(1)} %slice.73.own_ref), channel_id=1, source_target_pairs={{0,12},{4,0},{8,4},{12,8},{16,28},{20,16},{24,20},{28,24},{32,44},... | collective-permute-start | bytes 589832 | tf_op jit(solution)/shard_map/columns/ppermute | solution.py:352
  130.5 9.7 %collective-permute-start.7 = (bf16[256,384]{1,0:T(8,128)(2,1)S(1)}, bf16[256,384]{1,0:T(8,128)(2,1)S(1)}, u32[]{:S(2)}, u32[]{:S(2)}) collective-permute-start(bf16[256,384]{1,0:T(8,128)(2,1)S(1)} %slice.73.own_ref), channel_id=1, source_target_pairs={{0,48},{4,52},{8,56},{12,60},{16,0},{20,4},{24,8},{28,12},{32,16},... | collective-permute-start | bytes 589832 | tf_op jit(solution)/shard_map/columns/ppermute | solution.py:356
  131.8 8.4 %collective-permute-start.8 = (bf16[256,384]{1,0:T(8,128)(2,1)S(1)}, bf16[256,384]{1,0:T(8,128)(2,1)S(1)}, u32[]{:S(2)}, u32[]{:S(2)}) collective-permute-start(bf16[256,384]{1,0:T(8,128)(2,1)S(1)} %slice.73.own_ref), channel_id=1, source_target_pairs={{0,32},{4,36},{8,40},{12,44},{16,48},{20,52},{24,56},{28,60},{32,0... | collective-permute-start | bytes 589832 | tf_op jit(solution)/shard_map/columns/ppermute | solution.py:356
  134.6 9.2 %collective-permute-start.9 = (bf16[256,384]{1,0:T(8,128)(2,1)S(1)}, bf16[256,384]{1,0:T(8,128)(2,1)S(1)}, u32[]{:S(2)}, u32[]{:S(2)}) collective-permute-start(bf16[256,384]{1,0:T(8,128)(2,1)S(1)} %slice.73.own_ref), channel_id=1, source_target_pairs={{0,16},{4,20},{8,24},{12,28},{16,32},{20,36},{24,40},{28,44},{32,4... | collective-permute-start | bytes 589832 | tf_op jit(solution)/shard_map/columns/ppermute | solution.py:356
  146.7 32.6 %copy-start.16 = (s32[6,3,128]{2,1,0:T(4,128)S(1)}, s32[6,3,128]{2,1,0:T(4,128)}, u32[]{:S(2)}) copy-start(s32[6,3,128]{2,1,0:T(4,128)} %param.12) | copy-start | bytes 27652
  161.6 6.9 %collective-permute-start.10 = (bf16[256,384]{1,0:T(8,128)(2,1)S(1)}, bf16[256,384]{1,0:T(8,128)(2,1)S(1)}, u32[]{:S(2)}, u32[]{:S(2)}) collective-permute-start(bf16[256,384]{1,0:T(8,128)(2,1)S(1)} %get-tuple-element.37), channel_id=1, source_target_pairs={{0,12},{4,0},{8,4},{12,8},{16,28},{20,16},{24,20},{28,24},{32,44},... | collective-permute-start | bytes 589832 | tf_op jit(solution)/shard_map/schur/ppermute | solution.py:352
  162.0 8.7 %collective-permute-start.11 = (bf16[256,384]{1,0:T(8,128)(2,1)S(1)}, bf16[256,384]{1,0:T(8,128)(2,1)S(1)}, u32[]{:S(2)}, u32[]{:S(2)}) collective-permute-start(bf16[256,384]{1,0:T(8,128)(2,1)S(1)} %get-tuple-element.38), channel_id=1, source_target_pairs={{0,8},{4,12},{8,0},{12,4},{16,24},{20,28},{24,16},{28,20},{32,40},... | collective-permute-start | bytes 589832 | tf_op jit(solution)/shard_map/schur/ppermute | solution.py:352
  164.2 8.6 %collective-permute-start.12 = (bf16[256,384]{1,0:T(8,128)(2,1)S(1)}, bf16[256,384]{1,0:T(8,128)(2,1)S(1)}, u32[]{:S(2)}, u32[]{:S(2)}) collective-permute-start(bf16[256,384]{1,0:T(8,128)(2,1)S(1)} %get-tuple-element.39), channel_id=1, source_target_pairs={{0,4},{4,8},{8,12},{12,0},{16,20},{20,24},{24,28},{28,16},{32,36},... | collective-permute-start | bytes 589832 | tf_op jit(solution)/shard_map/schur/ppermute | solution.py:352
  174.8 22.3 %all-to-all-start.4 = ((f32[16,24,640]{2,1,0:T(8,128)}), f32[16,24,640]{2,1,0:T(8,128)}, u32[]{:S(2)}, u32[]{:S(2)}) async-start(f32[16,24,640]{2,1,0:T(8,128)} %broadcast_in_dim.12), calls=%async_computation.4 | async-start | bytes 1966080 | tf_op jit(solution)/shard_map/schur/all_to_all | solution.py:454
  179.4 3.2 %copy-start.8 = (bf16[1792,2048]{1,0:T(8,128)(2,1)S(1)}, bf16[1792,2048]{1,0:T(8,128)(2,1)}, u32[]{:S(2)}) copy-start(bf16[1792,2048]{1,0:T(8,128)(2,1)} %all-gather.5.cloned.1.call-done) | copy-start | bytes 22020100
  182.6 1.9 copy-start.10
  197.1 1.0 copy-start.3
  198.0 0.7 copy-start.5
  213.8 12.4 %copy-start.12 = (f32[384,384]{1,0:T(8,128)}, f32[384,384]{1,0:T(8,128)S(1)}, u32[]{:S(2)}) copy-start(f32[384,384]{1,0:T(8,128)S(1)} %get-tuple-element.42.inv_ref) | copy-start | bytes 1769476
  228.4 4.7 %copy-start.17 = (s32[6,3,128]{2,1,0:T(4,128)S(1)}, s32[6,3,128]{2,1,0:T(4,128)}, u32[]{:S(2)}) copy-start(s32[6,3,128]{2,1,0:T(4,128)} %param.12) | copy-start | bytes 27652
  228.4 5.1 %copy-start.6 = (s32[1,1,3,128]{3,1,2,0:T(1,128)S(1)}, s32[1,1,3,128]{3,1,2,0:T(1,128)}, u32[]{:S(2)}) copy-start(s32[1,1,3,128]{3,1,2,0:T(1,128)} %copy-done.4) | copy-start | bytes 4612
  228.5 5.1 %copy-start.13 = (f32[384,384]{1,0:T(8,128)S(1)}, f32[384,384]{1,0:T(8,128)}, u32[]{:S(2)}) copy-start(f32[384,384]{1,0:T(8,128)} %copy-done.12) | copy-start | bytes 1769476
  228.5 42.9 %all-to-all-start.6 = ((bf16[16,3,16,2048]{3,2,1,0:T(8,128)(2,1)}), bf16[16,3,16,2048]{3,2,1,0:T(8,128)(2,1)}, u32[]{:S(2)}, u32[]{:S(2)}) async-start(bf16[16,3,16,2048]{3,2,1,0:T(8,128)(2,1)} %signal.1), calls=%async_computation.6 | async-start | bytes 6291456 | tf_op jit(solution)/shard_map/signal/all_to_all | solution.py:471
  233.6 1.9 copy-start.11
  238.7 32.6 %collective-permute-start.13 = (bf16[256,1024]{1,0:T(8,128)(2,1)S(1)}, bf16[256,1024]{1,0:T(8,128)(2,1)S(1)}, u32[]{:S(2)}, u32[]{:S(2)}) collective-permute-start(bf16[256,1024]{1,0:T(8,128)(2,1)S(1)} %get-tuple-element.44), channel_id=1, source_target_pairs={{0,1},{1,2},{2,3},{3,0},{4,5},{5,6},{6,7},{7,4},{8,9},{9,10},{10,1... | collective-permute-start | bytes 1572872 | tf_op jit(solution)/shard_map/update/ppermute | solution.py:359
  239.4 32.0 %collective-permute-start.14 = (bf16[256,1024]{1,0:T(8,128)(2,1)S(1)}, bf16[256,1024]{1,0:T(8,128)(2,1)S(1)}, u32[]{:S(2)}, u32[]{:S(2)}) collective-permute-start(bf16[256,1024]{1,0:T(8,128)(2,1)S(1)} %get-tuple-element.45), channel_id=1, source_target_pairs={{0,2},{1,3},{2,0},{3,1},{4,6},{5,7},{6,4},{7,5},{8,10},{9,11},{10,... | collective-permute-start | bytes 1572872 | tf_op jit(solution)/shard_map/update/ppermute | solution.py:359
  241.5 29.9 %collective-permute-start.15 = (bf16[256,1024]{1,0:T(8,128)(2,1)S(1)}, bf16[256,1024]{1,0:T(8,128)(2,1)}, u32[]{:S(2)}, u32[]{:S(2)}) collective-permute-start(bf16[256,1024]{1,0:T(8,128)(2,1)S(1)} %get-tuple-element.46), channel_id=1, source_target_pairs={{0,3},{1,0},{2,1},{3,2},{4,7},{5,4},{6,5},{7,6},{8,11},{9,8},{10,9... | collective-permute-start | bytes 1572872 | tf_op jit(solution)/shard_map/update/ppermute | solution.py:359
  274.7 14.1 %all-to-all-start.7 = ((f32[64,1,3]{2,1,0:T(1,128)}), f32[64,1,3]{2,1,0:T(1,128)S(1)}, u32[]{:S(2)}, u32[]{:S(2)}) async-start(f32[64,1,3]{2,1,0:T(1,128)} %broadcast_in_dim.13), calls=%async_computation.7 | async-start | bytes 65536 | tf_op jit(solution)/shard_map/signal/all_to_all | solution.py:476
  282.8 6.9 %copy-start.1 = (bf16[3,1024,256]{2,1,0:T(8,128)(2,1)S(1)}, bf16[3,1024,256]{2,1,0:T(8,128)(2,1)}, u32[]{:S(2)}) copy-start(bf16[3,1024,256]{2,1,0:T(8,128)(2,1)} %param.13) | copy-start | bytes 4718596
Sparse Core Ops, SparseCore 0:
  12.3 68.3 all-gather.4
  173.7 50.6 all-gather.6

commit v2 on v1

--- a/solution.py
+++ b/solution.py
@@ -25,8 +25,8 @@
 HBM = pl.BlockSpec(memory_space=pltpu.HBM)
 
 
-def params():
-    return pltpu.CompilerParams(vmem_limit_bytes=40 * 1024 * 1024)
+def params(mib=40):
+    return pltpu.CompilerParams(vmem_limit_bytes=mib * 1024 * 1024)
 
 
 def cost(flops, nbytes):
@@ -66,35 +66,40 @@
     return (ids == place_ref[g]).astype(f32).astype(bf16)
 
 
-def start_inputs(gathered_ref, channel_ref, window_ref, held_ref, sems, groups, per_group):
+def start_inputs(gathered_ref, channel_ref, window_ref, held_ref, sems, row=None):
+    groups, user_rows = channel_ref.shape[:2]
     copies = []
     for g in range(groups):
-        start = g * per_group // 16 * 16
-        window = pltpu.make_async_copy(
-            gathered_ref.at[:, pl.ds(start, WINDOW), :], window_ref.at[g], sems.at[0, g]
-        )
-        channel = pltpu.make_async_copy(channel_ref.at[g], held_ref.at[g], sems.at[1, g])
-        window.start()
-        channel.start()
-        copies.append((window, channel))
+        start = g * 2 * EPOCHS * 6 // 16 * 16
+        source = gathered_ref.at[:, pl.ds(start, WINDOW), :]
+        parts = [
+            pltpu.make_async_copy(channel_ref.at[g], held_ref.at[g, :user_rows], sems.at[0, g]),
+            pltpu.make_async_copy(source, window_ref.at[g], sems.at[1, g]),
+        ]
+        if row is not None:
+            source = gathered_ref.at[row, pl.ds(start, WINDOW), :]
+            parts.append(
+                pltpu.make_async_copy(source, held_ref.at[g, user_rows:], sems.at[2, g])
+            )
+        for part in parts:
+            part.start()
+        copies.append(parts)
     return copies
 
 
-def input_scratch(groups, user_rows, antennas):
+def input_scratch(groups, rows, antennas):
     return [
         pltpu.VMEM((groups, 16, WINDOW, antennas), bf16),
-        pltpu.VMEM((groups, user_rows, antennas), bf16),
-        pltpu.SemaphoreType.DMA((2, groups)),
+        pltpu.VMEM((groups, rows, antennas), bf16),
+        pltpu.SemaphoreType.DMA((3, groups)),
     ]
 
 
 def columns_kernel(
     row_ref, gathered_ref, channel_ref, place_ref, out_ref, window_ref, held_ref, sems
 ):
-    groups, user_rows, antennas = held_ref.shape
-    copies = start_inputs(
-        gathered_ref, channel_ref, window_ref, held_ref, sems, groups, 2 * EPOCHS * 6
-    )
+    groups, _, antennas = channel_ref.shape
+    copies = start_inputs(gathered_ref, channel_ref, window_ref, held_ref, sems, row_ref[0])
     out_ref[groups] = jnp.zeros(out_ref.shape[1:], bf16)
     for g in range(groups):
         choose = choosing(place_ref, g)
@@ -102,9 +107,7 @@
             copy.wait()
         window = window_ref[g].reshape(16 * WINDOW, antennas)
         wide = dot_t(held_ref[g], window).astype(bf16)
-        out_ref[g, :user_rows] = dot(wide, choose).astype(bf16)
-        wide = dot_t(window_ref[g, row_ref[0]], window).astype(bf16)
-        out_ref[g, user_rows:] = dot(wide, choose).astype(bf16)
+        out_ref[g] = dot(wide, choose).astype(bf16)
 
 
 def make_columns(row, gathered, channels, place):
@@ -114,8 +117,8 @@
         out_shape=jax.ShapeDtypeStruct((groups + 1, user_rows + WINDOW, TOTAL), bf16),
         in_specs=[SMEM, HBM, HBM, VMEM],
         out_specs=VMEM,
-        scratch_shapes=input_scratch(groups, user_rows, antennas),
-        compiler_params=params(),
+        scratch_shapes=input_scratch(groups, user_rows + WINDOW, antennas),
+        compiler_params=params(60),
         cost_estimate=cost(4_000_000_000, 12_000_000),
         name="columns",
     )(row, gathered, channels, place)
@@ -124,10 +127,8 @@
 def channel_kernel(
     first_ref, gathered_ref, channel_ref, place_ref, slots_ref, out_ref, window_ref, held_ref, sems
 ):
-    groups, user_rows, antennas = held_ref.shape
-    copies = start_inputs(
-        gathered_ref, channel_ref, window_ref, held_ref, sems, groups, 2 * EPOCHS * 6
-    )
+    groups, user_rows, antennas = channel_ref.shape
+    copies = start_inputs(gathered_ref, channel_ref, window_ref, held_ref, sems)
     for g in range(groups):
         here = placing(slots_ref.at[g], first_ref[0], user_rows).astype(bf16)
         route = dot_t(here, choosing(place_ref, g)).astype(bf16)
@@ -145,7 +146,7 @@
         in_specs=[SMEM, HBM, HBM, VMEM, VMEM],
         out_specs=VMEM,
         scratch_shapes=input_scratch(groups, user_rows, antennas),
-        compiler_params=params(),
+        compiler_params=params(60),
         cost_estimate=cost(4_000_000_000, 14_000_000),
         name="channel",
     )(first, gathered, channels, place, slots_mine)
@@ -414,15 +415,15 @@
         ).reshape(1, TOTAL)
 
     with jax.named_scope("columns"):
-        gathered, full_rows, precoded = lax.optimization_barrier(
-            (gathered, full_rows, precoded)
-        )
         squares = []
         for d in range(4):
             piece = lax.dynamic_index_in_dim(full_rows, (x_index + d) % 4, 1, keepdims=False)
-            squares.append(along_x(piece, d) if d else piece)
+            squares.append(along_x(piece, d) if d in (1, 3) else piece)
+        gathered, squares, precoded = lax.optimization_barrier((gathered, squares, precoded))
+        squares[2] = along_x(squares[2], 2)
         both = make_columns(row_index.reshape(1), gathered, channels, place)
         both = lax.all_to_all(both, "col", 0, 0, tiled=True)
+        both, squares = lax.optimization_barrier((both, squares))
         summed = jnp.sum(both.astype(f32), axis=0)
         columns = summed[:user_rows]
         gram = summed[user_rows:]
@@ -437,12 +438,6 @@
         )
         packed = packed.reshape(16, SHARE, TOTAL + STREAMS)
         shared = lax.all_to_all(packed, "row", 0, 0, tiled=True)
-        shared, block1, block2, block3 = lax.optimization_barrier(
-            (shared, block1, block2, block3)
-        )
-        weighted = block0
-        for d, block in ((1, block1), (2, block2), (3, block3)):
-            weighted = weighted + along_x(block, -d).astype(f32)
         shared = jnp.sum(shared.astype(f32), axis=0)
         share_ids = row_index * SHARE + jnp.arange(SHARE, dtype=jnp.int32)
         identity = loading * (
@@ -452,11 +447,15 @@
         ready = jnp.concatenate([schur_rows, shared[:, TOTAL:]], axis=1)
         ready = jnp.broadcast_to(ready[None], (16, SHARE, TOTAL + STREAMS))
         whole = lax.all_to_all(ready, "row", 0, 0, tiled=True).reshape(TOTAL, TOTAL + STREAMS)
+        ready, block1, block2, block3 = lax.optimization_barrier((ready, block1, block2, block3))
+        weighted = block0
+        for d, block in ((1, block1), (2, block2), (3, block3)):
+            weighted = weighted + along_x(block, -d).astype(f32)
 
     with jax.named_scope("users"):
+        channel = make_channel(first_arg, gathered, channels, place, slots_mine)
+        whole, channel, weighted = lax.optimization_barrier((whole, channel, weighted))
         weighted_all = lax.all_gather(weighted.astype(bf16), "row")
-        channel = make_channel(first_arg, gathered, channels, place, slots_mine)
-        whole, channel = lax.optimization_barrier((whole, channel))
         schur_inverse, users = make_solve(first_arg, whole, weighted, precoded, slot_plane)
         users_side = lax.all_to_all(users, "col", 0, 0, tiled=True)
 

time: 298 us -> 325 us (1.091)
  waiting for transfers between devices: 116 us -> 156 us
  blocking collectives: 27.2 us -> 11.7 us
  local copies, waits for them, and re-layouts: 28.2 us -> 18.3 us
  starting transfers between devices: 51.5 us -> 61.4 us
    all_gather x1, waiting for transfers between devices: 0.02 us -> 43.8 us  [local(): weighted_all = lax.all_gather(weighted.astype(bf16), 'row')]
    all_to_all x1, waiting for transfers between devices: 26.8 us -> 0.01 us  [local(): received = lax.all_to_all(signal_part, 'row', 0, 0, tiled=True)]
    ppermute x9, waiting for transfers between devices: 16.8 us -> 36 us  [along_x(): return lax.ppermute(value, 'row', pairs)]
    ppermute x3, waiting for transfers between devices: 0.01 us -> 18.5 us  [along_z(): return lax.ppermute(value, 'col', [(z, (z + step) % 4) for z in range(4)])]
    all_to_all x1 -> x0, blocking collectives: 14.8 us -> none  [local(): shared = lax.all_to_all(packed, 'row', 0, 0, tiled=True)]
    unnamed x47 -> x29, local copies, waits for them, and re-layouts: 18.6 us -> 8.06 us
    all_to_all x0 -> x1, waiting for transfers between devices: none -> 9.91 us  [local(): shared = lax.all_to_all(packed, 'row', 0, 0, tiled=True)]
    all_to_all x1, waiting for transfers between devices: 7.8 us -> 0.01 us  [local(): lax.all_to_all(ready, 'row', 0, 0, tiled=True)]
  transfers between devices with their start and end apart: 24 -> 25, of which waited for: 14 -> 18; matrix products, arithmetic and copies ran while one was open for 9% -> 8% of each run, Pallas kernels for 9% -> 8%
where the time goes in v2:
time: 325 us; the launch traced here: 324 us
  waiting for transfers between devices  156 us (48%)
  starting transfers between devices  61.4 us (19%)
  Pallas kernels  40.8 us (13%)
  local copies, waits for them, and re-layouts  18.3 us (6%)
  other arithmetic  17.6 us (5%)
  between operations  14.5 us (4%)
  blocking collectives  11.7 us (4%)
  matrix products  3.64 us (1%)
    all_gather x1, waiting for transfers between devices, local(): weighted_all = lax.all_gather(weighted.astype(bf16), 'row')  43.8 us
    ppermute x9, waiting for transfers between devices, along_x(): return lax.ppermute(value, 'row', pairs)  36 us
    all_to_all x2, waiting for transfers between devices, to_planes(): return lax.all_to_all(padded, 'col', 0, 0, tiled=True)  29.9 us
    ppermute x3, waiting for transfers between devices, along_z(): return lax.ppermute(value, 'col', [(z, (z + step) % 4) for z in range(4)])  18.5 us
    pallas_call x1, Pallas kernels, make_solve(): pl.pallas_call(solve_kernel, out_shape=(jax.ShapeDtypeStruct((TOTAL, TOTA...  13.9 us
    ppermute x9, starting transfers between devices, along_x(): return lax.ppermute(value, 'row', pairs)  13.7 us
    all_to_all x1, blocking collectives, local(): users_side = lax.all_to_all(users, 'col', 0, 0, tiled=True)  11.7 us
    all_to_all x1, waiting for transfers between devices, local(): shared = lax.all_to_all(packed, 'row', 0, 0, tiled=True)  9.91 us
  transfers between devices with their start and end apart: 25, of which 18 were waited for; matrix products, arithmetic and copies ran while one was open for 8% of the time, Pallas kernels for 8%

profile of v2, /device:TPU:0, one launch (start us, length us, event | category | flops | bytes accessed | tf_op | source)
XLA Modules:
  0.0 323.9 jit_solution(2873197720115616058)
XLA Ops:
  7.2 1.1 constant_dynamic-slice_fusion.3
  8.4 1.6 collective-permute-done
  10.0 1.0 select_bitcast_fusion.1
  11.3 0.8 pad.6
  12.2 3.0 copy.24
  15.2 1.7 copy.29
  16.9 1.5 concatenate.9.clone
  18.4 5.4 %all-to-all-start = ((bf16[4,4,256,256]{3,2,1,0:T(8,128)(2,1)}), bf16[4,4,256,256]{3,2,1,0:T(8,128)(2,1)}, u32[]{:S(2)}, u32[]{:S(2)}) async-start(bf16[4,4,256,256]{3,2,1,0:T(8,128)(2,1)} %concatenate.9.clone), calls=%async_computation | async-start | bytes 4194304 | tf_op jit(solution)/shard_map/planes/all_to_all | solution.py:364
  24.1 3.6 %fusion.14 = f32[3,256,256]{2,1,0:T(8,128)S(1)} fusion(f32[3,256,1024]{2,1,0:T(8,128)} %param.8, bf16[3,1024,256]{2,1,0:T(8,128)(2,1)S(1)} %copy-done), kind=kOutput, calls=%fused_computation.66 | convolution fusion | flops 2415919104 | bytes 5505024 | tf_op jit(solution)/shard_map/planes/grc,gcs->grs/dot_general | solution.py:386
  27.8 1.1 concatenate.10
  28.8 21.9 %all-to-all-done = bf16[4,4,256,256]{3,2,1,0:T(8,128)(2,1)} async-done(((bf16[4,4,256,256]{3,2,1,0:T(8,128)(2,1)}), bf16[4,4,256,256]{3,2,1,0:T(8,128)(2,1)}, u32[]{:S(2)}, u32[]{:S(2)}) %all-to-all-start) | async-done | bytes 2097184 | tf_op jit(solution)/shard_map/planes/all_to_all | solution.py:364
  50.7 4.2 %all-to-all-start.1 = ((f32[4,256,256]{2,1,0:T(8,128)}), f32[4,256,256]{2,1,0:T(8,128)}, u32[]{:S(2)}, u32[]{:S(2)}) async-start(f32[4,256,256]{2,1,0:T(8,128)} %concatenate.10), calls=%async_computation.1 | async-start | bytes 2097152 | tf_op jit(solution)/shard_map/planes/all_to_all | solution.py:364
  55.1 2.5 dynamic-slice_bitcast_fusion
  57.6 1.5 collective-permute-start.1
  59.1 1.7 collective-permute-start.2
  61.7 8.0 %all-to-all-done.1 = f32[4,256,256]{2,1,0:T(8,128)} async-done(((f32[4,256,256]{2,1,0:T(8,128)}), f32[4,256,256]{2,1,0:T(8,128)}, u32[]{:S(2)}, u32[]{:S(2)}) %all-to-all-start.1) | async-done | bytes 1048608 | tf_op jit(solution)/shard_map/planes/all_to_all | solution.py:364
  69.6 1.3 reduce_sum.76.precoded_ref
  70.9 13.5 %collective-permute-done.1.square1_ref = bf16[4,256,256]{2,1,0:T(8,128)(2,1)S(1)} collective-permute-done((bf16[4,256,256]{2,1,0:T(8,128)(2,1)}, bf16[4,256,256]{2,1,0:T(8,128)(2,1)S(1)}, u32[]{:S(2)}, u32[]{:S(2)}) %collective-permute-start.1) | collective-permute-done | bytes 524320 | tf_op jit(solution)/shard_map/columns/ppermute | solution.py:353
  84.4 7.5 %all-gather.5.cloned.1.call-done = bf16[1792,2048]{1,0:T(8,128)(2,1)} async-done(((bf16[112,2048]{1,0:T(8,128)(2,1)}), bf16[1792,2048]{1,0:T(8,128)(2,1)}) %all-gather.5.cloned.1.call-update) | async-done | bytes 7340048 | tf_op jit(solution)/shard_map/newcomers/all_gather | solution.py:381
  91.9 9.7 %columns.1 = bf16[4,304,384]{2,1,0:T(8,128)(2,1)} custom-call(s32[1]{0:T(128)} %bitcast.3.row_ref, bf16[16,112,2048]{2,1,0:T(8,128)(2,1)} %bitcast.75, bf16[3,256,2048]{2,1,0:T(8,128)(2,1)} %channel_ref.3, s32[3,1,384]{2,1,0:T(1,128)} %fusion.10.place_ref), custom_call_target="tpu_custom_call" | custom-call | flops 4000000000 | bytes 12000000 | tf_op jit(solution)/shard_map/columns/columns/pallas_call | solution.py:115
  101.7 4.4 %all-to-all-start.2 = ((bf16[4,304,384]{2,1,0:T(8,128)(2,1)}), bf16[4,304,384]{2,1,0:T(8,128)(2,1)}, u32[]{:S(2)}, u32[]{:S(2)}) async-start(bf16[4,304,384]{2,1,0:T(8,128)(2,1)} %columns.1), calls=%async_computation.2 | async-start | bytes 1867776 | tf_op jit(solution)/shard_map/columns/all_to_all | solution.py:425
  106.1 1.5 collective-permute-start.3
  107.6 13.6 %collective-permute-done.3.square2_ref = bf16[4,256,256]{2,1,0:T(8,128)(2,1)S(1)} collective-permute-done((bf16[4,256,256]{2,1,0:T(8,128)(2,1)S(1)}, bf16[4,256,256]{2,1,0:T(8,128)(2,1)S(1)}, u32[]{:S(2)}, u32[]{:S(2)}) %collective-permute-start.3) | collective-permute-done | bytes 524320 | tf_op jit(solution)/shard_map/columns/ppermute | solution.py:353
  121.1 1.4 convert_reduce_fusion.1
  122.9 2.0 collective-permute-start.5
  124.9 1.8 collective-permute-start.6
  126.8 2.7 collective-permute-start.7
  129.5 0.8 collective-permute-start.8
  130.3 3.4 %collective-permute-done.4.row1_ref = bf16[256,384]{1,0:T(8,128)(2,1)S(1)} collective-permute-done((bf16[256,384]{1,0:T(8,128)(2,1)S(1)}, bf16[256,384]{1,0:T(8,128)(2,1)S(1)}, u32[]{:S(2)}, u32[]{:S(2)}) %collective-permute-start.4) | collective-permute-done | bytes 196640 | tf_op jit(solution)/shard_map/columns/ppermute | solution.py:353
  133.8 1.5 collective-permute-start.9
  136.2 2.1 collective-permute-done.8.col2_ref
  138.3 2.4 collective-permute-done.9.col3_ref
  140.6 3.7 %middle.1 = (f32[256,384]{1,0:T(8,128)S(1)}, bf16[256,384]{1,0:T(8,128)(2,1)S(1)}, bf16[256,384]{1,0:T(8,128)(2,1)S(1)}, bf16[256,384]{1,0:T(8,128)(2,1)S(1)}, bf16[384,640]{1,0:T(8,128)(2,1)}) custom-call(s32[3]{0:T(128)S(1)} %pad_add_fusion.where_ref, bf16[4,256,256]{2,1,0:T(8,128)(2,1)S(1)} %get-tuple-element.40.square0_ref, ...), custom_call_target="tpu_custom_call" | custom-call | flops 2000000000 | bytes 8000000 | tf_op jit(solution)/shard_map/schur/middle/pallas_call | solution.py:183
  145.7 3.7 %all-to-all-start.3 = ((bf16[16,24,640]{2,1,0:T(8,128)(2,1)}), bf16[16,24,640]{2,1,0:T(8,128)(2,1)S(1)}, u32[]{:S(2)}, u32[]{:S(2)}) async-start(bf16[16,24,640]{2,1,0:T(8,128)(2,1)} %bitcast.14), calls=%async_computation.3 | async-start | bytes 983040 | tf_op jit(solution)/shard_map/schur/all_to_all | solution.py:440
  149.4 9.9 %all-to-all-done.3 = bf16[16,24,640]{2,1,0:T(8,128)(2,1)S(1)} async-done(((bf16[16,24,640]{2,1,0:T(8,128)(2,1)}), bf16[16,24,640]{2,1,0:T(8,128)(2,1)S(1)}, u32[]{:S(2)}, u32[]{:S(2)}) %all-to-all-start.3) | async-done | bytes 491552 | tf_op jit(solution)/shard_map/schur/all_to_all | solution.py:440
  159.5 1.1 broadcast_in_dim.12
  160.6 3.6 %all-to-all-start.4 = ((f32[16,24,640]{2,1,0:T(8,128)}), f32[16,24,640]{2,1,0:T(8,128)S(1)}, u32[]{:S(2)}, u32[]{:S(2)}) async-start(f32[16,24,640]{2,1,0:T(8,128)} %broadcast_in_dim.12), calls=%async_computation.4 | async-start | bytes 1966080 | tf_op jit(solution)/shard_map/schur/all_to_all | solution.py:449
  164.9 3.0 collective-permute-start.10
  167.9 0.8 collective-permute-start.11
  168.8 0.9 collective-permute-start.12
  169.6 8.2 %channel.1.channel_ref = bf16[3,256,2048]{2,1,0:T(8,128)(2,1)} custom-call(s32[1]{0:T(128)} %bitcast.1.first_ref, bf16[16,112,2048]{2,1,0:T(8,128)(2,1)} %bitcast.76, bf16[3,256,2048]{2,1,0:T(8,128)(2,1)} %channel_ref.3, s32[3,1,384]{2,1,0:T(1,128)} %fusion.10.place_ref, s32[3,1,384]{2,1,0:T(1,128)} %reshape.281.slots_ref), custom_call_target="tpu_custom_call" | custom-call | flops 4000000000 | bytes 14000000 | tf_op jit(solution)/shard_map/users/channel/pallas_call | solution.py:143
  177.8 2.5 collective-permute-done.10
  180.3 1.8 collective-permute-done.11
  182.1 1.2 collective-permute-done.12
  183.4 0.7 convert_element_type.55
  184.2 13.9 %solve.1 = (f32[384,384]{1,0:T(8,128)S(1)}, bf16[4,256,256]{2,1,0:T(8,128)(2,1)S(1)}) custom-call(s32[1]{0:T(128)} %bitcast.1.first_ref, f32[384,640]{1,0:T(8,128)S(1)} %bitcast.66, f32[256,384]{1,0:T(8,128)S(1)} %convert_add_fusion.weighted_ref, f32[256,256]{1,0:T(8,128)S(1)} %reduce_sum.76.precoded_ref, s32[1,384]{1,0:T(1,128)S(1)} %bitcast.68), custom_call_target="tpu_custom_call" | custom-call | flops 10000000000 | bytes 4000000 | tf_op jit(solution)/shard_map/users/solve/pallas_call | solution.py:257
  198.1 11.7 %all_to_all.40.users_ref = bf16[4,256,256]{2,1,0:T(8,128)(2,1)S(1)} all-to-all(bf16[4,256,256]{2,1,0:T(8,128)(2,1)S(1)} %get-tuple-element.56), channel_id=1, replica_groups=mesh['grp'=2,'row'=16,'col'=4] {'col'}, dimensions={0} | all-to-all | bytes 1048576 | tf_op jit(solution)/shard_map/users/all_to_all | solution.py:460
  209.8 2.1 signal.1
  211.9 5.6 %all-to-all-start.6 = ((bf16[16,3,16,2048]{3,2,1,0:T(8,128)(2,1)}), bf16[16,3,16,2048]{3,2,1,0:T(8,128)(2,1)}, u32[]{:S(2)}, u32[]{:S(2)}) async-start(bf16[16,3,16,2048]{3,2,1,0:T(8,128)(2,1)} %signal.1), calls=%async_computation.6 | async-start | bytes 6291456 | tf_op jit(solution)/shard_map/signal/all_to_all | solution.py:470
  218.0 43.8 %all-gather.7.cloned.1.call-done = bf16[4096,384]{1,0:T(8,128)(2,1)} async-done(((bf16[256,384]{1,0:T(8,128)(2,1)}), bf16[4096,384]{1,0:T(8,128)(2,1)}) %all-gather.7.cloned.1.call-update) | async-done | bytes 3145744 | tf_op jit(solution)/shard_map/users/all_gather | solution.py:458
  261.9 1.9 copy-done.3
  263.7 3.2 %update.1 = (bf16[256,1024]{1,0:T(8,128)(2,1)S(1)}, bf16[256,1024]{1,0:T(8,128)(2,1)S(1)}, bf16[256,1024]{1,0:T(8,128)(2,1)S(1)}, bf16[256,1024]{1,0:T(8,128)(2,1)S(1)}) custom-call(s32[2]{0:T(128)S(1)} %pad_add_fusion.1.where_ref, f32[256,384]{1,0:T(8,128)S(1)} %convert_add_fusion.weighted_ref, f32[384,384]{1,0:T(8,128)S(1)} %get-tuple-element.58.inv_ref, ...), custom_call_target="tpu_custom_call" | custom-call | flops 1500000000 | bytes 8000000 | tf_op jit(solution)/shard_map/update/update/pallas_call | solution.py:326
  267.0 1.3 collective-permute-start.13
  268.3 2.1 collective-permute-start.14
  270.5 2.2 collective-permute-start.15
  272.9 2.1 and_select_fusion
  274.9 6.5 %collective-permute-done.13 = bf16[256,1024]{1,0:T(8,128)(2,1)S(1)} collective-permute-done((bf16[256,1024]{1,0:T(8,128)(2,1)S(1)}, bf16[256,1024]{1,0:T(8,128)(2,1)S(1)}, u32[]{:S(2)}, u32[]{:S(2)}) %collective-permute-start.13) | collective-permute-done | bytes 524320 | tf_op jit(solution)/shard_map/update/ppermute | solution.py:360
  281.4 12.0 %collective-permute-done.14 = bf16[256,1024]{1,0:T(8,128)(2,1)} collective-permute-done((bf16[256,1024]{1,0:T(8,128)(2,1)S(1)}, bf16[256,1024]{1,0:T(8,128)(2,1)}, u32[]{:S(2)}, u32[]{:S(2)}) %collective-permute-start.14) | collective-permute-done | bytes 524320 | tf_op jit(solution)/shard_map/update/ppermute | solution.py:360
  293.5 2.5 convert_reduce_fusion
  296.8 9.8 %all-to-all-start.7 = ((f32[64,1,3]{2,1,0:T(1,128)}), f32[64,1,3]{2,1,0:T(1,128)S(1)}, u32[]{:S(2)}, u32[]{:S(2)}) async-start(f32[64,1,3]{2,1,0:T(1,128)} %broadcast_in_dim.13), calls=%async_computation.7 | async-start | bytes 65536 | tf_op jit(solution)/shard_map/signal/all_to_all | solution.py:475
  306.6 3.6 %fusion.8 = (f32[1,256,1024]{2,1,0:T(8,128)S(1)}, f32[1,256,1024]{2,1,0:T(8,128)S(1)}, f32[1,256,1024]{2,1,0:T(8,128)S(1)}) fusion(f32[3,256,1024]{2,1,0:T(8,128)} %and_select_fusion, f32[3,256,1024]{2,1,0:T(8,128)} %param.8, bf16[256,1024]{1,0:T(8,128)(2,1)} %collective-permute-done.15, bf16[256,1024]{1,0:T(8,128)(2,1)} %collective-permute-done.14, ...), kind=kLoop, calls=%fused_computation.16 | loop fusion | flops 4718592 | bytes 11534345 | tf_op jit(solution)/shard_map/final/stack | solution.py:492
  310.3 1.9 pad_maximum_fusion
  312.1 4.0 %all-to-all-done.7 = f32[64,1,3]{2,1,0:T(1,128)S(1)} async-done(((f32[64,1,3]{2,1,0:T(1,128)}), f32[64,1,3]{2,1,0:T(1,128)S(1)}, u32[]{:S(2)}, u32[]{:S(2)}) %all-to-all-start.7) | async-done | bytes 800 | tf_op jit(solution)/shard_map/signal/all_to_all | solution.py:475
  316.2 0.8 multiply_bitcast_fusion
  (76 shorter events, 6.7 us)
Async XLA Ops:
  7.2 17.0 %copy-start = (bf16[3,1024,256]{2,1,0:T(8,128)(2,1)S(1)}, bf16[3,1024,256]{2,1,0:T(8,128)(2,1)}, u32[]{:S(2)}) copy-start(bf16[3,1024,256]{2,1,0:T(8,128)(2,1)} %param.13) | copy-start | bytes 4718596
  7.2 84.8 %all-gather.5.cloned.1.call-start = ((), (), s32[]{:S(2)}) async-start(), calls=%async_computation.8 | async-start | bytes 7798784 | tf_op jit(solution)/shard_map/newcomers/all_gather | solution.py:381
  8.3 1.7 collective-permute-start
  16.9 6.9 %copy-start.9 = (s32[6,3,128,1]{2,3,1,0:T(1,128)S(1)}, s32[6,3,128,1]{2,3,1,0:T(1,128)}, u32[]{:S(2)}) copy-start(s32[6,3,128,1]{2,3,1,0:T(1,128)} %param.10) | copy-start | bytes 27652
  18.4 32.3 %all-to-all-start = ((bf16[4,4,256,256]{3,2,1,0:T(8,128)(2,1)}), bf16[4,4,256,256]{3,2,1,0:T(8,128)(2,1)}, u32[]{:S(2)}, u32[]{:S(2)}) async-start(bf16[4,4,256,256]{3,2,1,0:T(8,128)(2,1)} %concatenate.9.clone), calls=%async_computation | async-start | bytes 4194304 | tf_op jit(solution)/shard_map/planes/all_to_all | solution.py:364
  27.8 27.2 %copy-start.10 = (s32[32]{0:T(128)S(1)}, s32[32]{0:T(128)}, u32[]{:S(2)}) copy-start(s32[32]{0:T(128)} %param.11) | copy-start | bytes 388
  50.7 18.9 %all-to-all-start.1 = ((f32[4,256,256]{2,1,0:T(8,128)}), f32[4,256,256]{2,1,0:T(8,128)}, u32[]{:S(2)}, u32[]{:S(2)}) async-start(f32[4,256,256]{2,1,0:T(8,128)} %concatenate.10), calls=%async_computation.1 | async-start | bytes 2097152 | tf_op jit(solution)/shard_map/planes/all_to_all | solution.py:364
  57.6 26.8 %collective-permute-start.1 = (bf16[4,256,256]{2,1,0:T(8,128)(2,1)}, bf16[4,256,256]{2,1,0:T(8,128)(2,1)S(1)}, u32[]{:S(2)}, u32[]{:S(2)}) collective-permute-start(bf16[4,256,256]{2,1,0:T(8,128)(2,1)} %get-tuple-element.73), channel_id=1, source_target_pairs={{0,4},{4,8},{8,12},{12,0},{16,20},{20,24},{24,28},{28,16},{32,36},... | collective-permute-start | bytes 1572872 | tf_op jit(solution)/shard_map/columns/ppermute | solution.py:353
  59.1 25.3 %collective-permute-start.2 = (bf16[4,256,256]{2,1,0:T(8,128)(2,1)S(1)}, bf16[4,256,256]{2,1,0:T(8,128)(2,1)S(1)}, u32[]{:S(2)}, u32[]{:S(2)}) collective-permute-start(bf16[4,256,256]{2,1,0:T(8,128)(2,1)S(1)} %get-tuple-element.71), channel_id=1, source_target_pairs={{0,12},{4,0},{8,4},{12,8},{16,28},{20,16},{24,20},{28,24},{32,44},... | collective-permute-start | bytes 1572872 | tf_op jit(solution)/shard_map/columns/ppermute | solution.py:353
  101.6 21.2 %copy-start.8 = (s32[6,3,128]{2,1,0:T(4,128)S(1)}, s32[6,3,128]{2,1,0:T(4,128)}, u32[]{:S(2)}) copy-start(s32[6,3,128]{2,1,0:T(4,128)} %param.12) | copy-start | bytes 27652
  101.7 19.5 %all-to-all-start.2 = ((bf16[4,304,384]{2,1,0:T(8,128)(2,1)}), bf16[4,304,384]{2,1,0:T(8,128)(2,1)}, u32[]{:S(2)}, u32[]{:S(2)}) async-start(bf16[4,304,384]{2,1,0:T(8,128)(2,1)} %columns.1), calls=%async_computation.2 | async-start | bytes 1867776 | tf_op jit(solution)/shard_map/columns/all_to_all | solution.py:425
  106.1 15.0 %collective-permute-start.3 = (bf16[4,256,256]{2,1,0:T(8,128)(2,1)S(1)}, bf16[4,256,256]{2,1,0:T(8,128)(2,1)S(1)}, u32[]{:S(2)}, u32[]{:S(2)}) collective-permute-start(bf16[4,256,256]{2,1,0:T(8,128)(2,1)S(1)} %get-tuple-element.38), channel_id=1, source_target_pairs={{0,8},{4,12},{8,0},{12,4},{16,24},{20,28},{24,16},{28,20},{32,40},... | collective-permute-start | bytes 1572872 | tf_op jit(solution)/shard_map/columns/ppermute | solution.py:353
  122.5 11.2 %collective-permute-start.4 = (bf16[256,384]{1,0:T(8,128)(2,1)S(1)}, bf16[256,384]{1,0:T(8,128)(2,1)S(1)}, u32[]{:S(2)}, u32[]{:S(2)}) collective-permute-start(bf16[256,384]{1,0:T(8,128)(2,1)S(1)} %slice.73.own_ref), channel_id=1, source_target_pairs={{0,4},{4,8},{8,12},{12,0},{16,20},{20,24},{24,28},{28,16},{32,36},... | collective-permute-start | bytes 589832 | tf_op jit(solution)/shard_map/columns/ppermute | solution.py:353
  122.9 13.1 %collective-permute-start.5 = (bf16[256,384]{1,0:T(8,128)(2,1)S(1)}, bf16[256,384]{1,0:T(8,128)(2,1)S(1)}, u32[]{:S(2)}, u32[]{:S(2)}) collective-permute-start(bf16[256,384]{1,0:T(8,128)(2,1)S(1)} %slice.73.own_ref), channel_id=1, source_target_pairs={{0,8},{4,12},{8,0},{12,4},{16,24},{20,28},{24,16},{28,20},{32,40},... | collective-permute-start | bytes 589832 | tf_op jit(solution)/shard_map/columns/ppermute | solution.py:353
  124.9 11.1 %collective-permute-start.6 = (bf16[256,384]{1,0:T(8,128)(2,1)S(1)}, bf16[256,384]{1,0:T(8,128)(2,1)S(1)}, u32[]{:S(2)}, u32[]{:S(2)}) collective-permute-start(bf16[256,384]{1,0:T(8,128)(2,1)S(1)} %slice.73.own_ref), channel_id=1, source_target_pairs={{0,12},{4,0},{8,4},{12,8},{16,28},{20,16},{24,20},{28,24},{32,44},... | collective-permute-start | bytes 589832 | tf_op jit(solution)/shard_map/columns/ppermute | solution.py:353
  126.8 9.4 %collective-permute-start.7 = (bf16[256,384]{1,0:T(8,128)(2,1)S(1)}, bf16[256,384]{1,0:T(8,128)(2,1)S(1)}, u32[]{:S(2)}, u32[]{:S(2)}) collective-permute-start(bf16[256,384]{1,0:T(8,128)(2,1)S(1)} %slice.73.own_ref), channel_id=1, source_target_pairs={{0,48},{4,52},{8,56},{12,60},{16,0},{20,4},{24,8},{28,12},{32,16},... | collective-permute-start | bytes 589832 | tf_op jit(solution)/shard_map/columns/ppermute | solution.py:357
  129.5 8.8 %collective-permute-start.8 = (bf16[256,384]{1,0:T(8,128)(2,1)S(1)}, bf16[256,384]{1,0:T(8,128)(2,1)S(1)}, u32[]{:S(2)}, u32[]{:S(2)}) collective-permute-start(bf16[256,384]{1,0:T(8,128)(2,1)S(1)} %slice.73.own_ref), channel_id=1, source_target_pairs={{0,32},{4,36},{8,40},{12,44},{16,48},{20,52},{24,56},{28,60},{32,0... | collective-permute-start | bytes 589832 | tf_op jit(solution)/shard_map/columns/ppermute | solution.py:357
  133.8 6.9 %collective-permute-start.9 = (bf16[256,384]{1,0:T(8,128)(2,1)S(1)}, bf16[256,384]{1,0:T(8,128)(2,1)S(1)}, u32[]{:S(2)}, u32[]{:S(2)}) collective-permute-start(bf16[256,384]{1,0:T(8,128)(2,1)S(1)} %slice.73.own_ref), channel_id=1, source_target_pairs={{0,16},{4,20},{8,24},{12,28},{16,32},{20,36},{24,40},{28,44},{32,4... | collective-permute-start | bytes 589832 | tf_op jit(solution)/shard_map/columns/ppermute | solution.py:357
  144.3 0.7 copy-start.4
  145.0 0.7 copy-start.6
  145.7 19.2 %copy-start.7 = (bf16[256,384]{1,0:T(8,128)(2,1)S(1)}, bf16[256,384]{1,0:T(8,128)(2,1)}, u32[]{:S(2)}) copy-start(bf16[256,384]{1,0:T(8,128)(2,1)} %copy-done.6) | copy-start | bytes 589828
  145.7 22.3 %copy-start.5 = (bf16[256,384]{1,0:T(8,128)(2,1)S(1)}, bf16[256,384]{1,0:T(8,128)(2,1)}, u32[]{:S(2)}) copy-start(bf16[256,384]{1,0:T(8,128)(2,1)} %copy-done.4) | copy-start | bytes 589828
  145.7 13.6 %all-to-all-start.3 = ((bf16[16,24,640]{2,1,0:T(8,128)(2,1)}), bf16[16,24,640]{2,1,0:T(8,128)(2,1)S(1)}, u32[]{:S(2)}, u32[]{:S(2)}) async-start(bf16[16,24,640]{2,1,0:T(8,128)(2,1)} %bitcast.14), calls=%async_computation.3 | async-start | bytes 983040 | tf_op jit(solution)/shard_map/schur/all_to_all | solution.py:440
  160.6 22.9 %all-to-all-start.4 = ((f32[16,24,640]{2,1,0:T(8,128)}), f32[16,24,640]{2,1,0:T(8,128)S(1)}, u32[]{:S(2)}, u32[]{:S(2)}) async-start(f32[16,24,640]{2,1,0:T(8,128)} %broadcast_in_dim.12), calls=%async_computation.4 | async-start | bytes 1966080 | tf_op jit(solution)/shard_map/schur/all_to_all | solution.py:449
  164.2 97.6 %all-gather.7.cloned.1.call-start = ((), (), s32[]{:S(2)}) async-start(), calls=%async_computation.9 | async-start | bytes 3342336 | tf_op jit(solution)/shard_map/users/all_gather | solution.py:458
  164.9 15.4 %collective-permute-start.10 = (bf16[256,384]{1,0:T(8,128)(2,1)S(1)}, bf16[256,384]{1,0:T(8,128)(2,1)S(1)}, u32[]{:S(2)}, u32[]{:S(2)}) collective-permute-start(bf16[256,384]{1,0:T(8,128)(2,1)S(1)} %copy-done.7), channel_id=1, source_target_pairs={{0,12},{4,0},{8,4},{12,8},{16,28},{20,16},{24,20},{28,24},{32,44},... | collective-permute-start | bytes 589832 | tf_op jit(solution)/shard_map/schur/ppermute | solution.py:353
  167.9 14.2 %collective-permute-start.11 = (bf16[256,384]{1,0:T(8,128)(2,1)S(1)}, bf16[256,384]{1,0:T(8,128)(2,1)S(1)}, u32[]{:S(2)}, u32[]{:S(2)}) collective-permute-start(bf16[256,384]{1,0:T(8,128)(2,1)S(1)} %copy-done.5), channel_id=1, source_target_pairs={{0,8},{4,12},{8,0},{12,4},{16,24},{20,28},{24,16},{28,20},{32,40},... | collective-permute-start | bytes 589832 | tf_op jit(solution)/shard_map/schur/ppermute | solution.py:353
  168.8 14.6 %collective-permute-start.12 = (bf16[256,384]{1,0:T(8,128)(2,1)S(1)}, bf16[256,384]{1,0:T(8,128)(2,1)S(1)}, u32[]{:S(2)}, u32[]{:S(2)}) collective-permute-start(bf16[256,384]{1,0:T(8,128)(2,1)S(1)} %get-tuple-element.53), channel_id=1, source_target_pairs={{0,4},{4,8},{8,12},{12,0},{16,20},{20,24},{24,28},{28,16},{32,36},... | collective-permute-start | bytes 589832 | tf_op jit(solution)/shard_map/schur/ppermute | solution.py:353
  184.2 25.6 %copy-start.2 = (bf16[3,256,2048]{2,1,0:T(8,128)(2,1)S(1)}, bf16[3,256,2048]{2,1,0:T(8,128)(2,1)}, u32[]{:S(2)}) copy-start(bf16[3,256,2048]{2,1,0:T(8,128)(2,1)} %channel.1.channel_ref) | copy-start | bytes 9437188
  211.9 63.0 %all-to-all-start.6 = ((bf16[16,3,16,2048]{3,2,1,0:T(8,128)(2,1)}), bf16[16,3,16,2048]{3,2,1,0:T(8,128)(2,1)}, u32[]{:S(2)}, u32[]{:S(2)}) async-start(bf16[16,3,16,2048]{3,2,1,0:T(8,128)(2,1)} %signal.1), calls=%async_computation.6 | async-start | bytes 6291456 | tf_op jit(solution)/shard_map/signal/all_to_all | solution.py:470
  261.8 1.9 copy-start.3
  267.0 14.4 %collective-permute-start.13 = (bf16[256,1024]{1,0:T(8,128)(2,1)S(1)}, bf16[256,1024]{1,0:T(8,128)(2,1)S(1)}, u32[]{:S(2)}, u32[]{:S(2)}) collective-permute-start(bf16[256,1024]{1,0:T(8,128)(2,1)S(1)} %get-tuple-element.60), channel_id=1, source_target_pairs={{0,1},{1,2},{2,3},{3,0},{4,5},{5,6},{6,7},{7,4},{8,9},{9,10},{10,1... | collective-permute-start | bytes 1572872 | tf_op jit(solution)/shard_map/update/ppermute | solution.py:360
  268.3 25.1 %collective-permute-start.14 = (bf16[256,1024]{1,0:T(8,128)(2,1)S(1)}, bf16[256,1024]{1,0:T(8,128)(2,1)}, u32[]{:S(2)}, u32[]{:S(2)}) collective-permute-start(bf16[256,1024]{1,0:T(8,128)(2,1)S(1)} %get-tuple-element.61), channel_id=1, source_target_pairs={{0,2},{1,3},{2,0},{3,1},{4,6},{5,7},{6,4},{7,5},{8,10},{9,11},{10,... | collective-permute-start | bytes 1572872 | tf_op jit(solution)/shard_map/update/ppermute | solution.py:360
  270.5 23.0 %collective-permute-start.15 = (bf16[256,1024]{1,0:T(8,128)(2,1)S(1)}, bf16[256,1024]{1,0:T(8,128)(2,1)}, u32[]{:S(2)}, u32[]{:S(2)}) collective-permute-start(bf16[256,1024]{1,0:T(8,128)(2,1)S(1)} %get-tuple-element.62), channel_id=1, source_target_pairs={{0,3},{1,0},{2,1},{3,2},{4,7},{5,4},{6,5},{7,6},{8,11},{9,8},{10,9... | collective-permute-start | bytes 1572872 | tf_op jit(solution)/shard_map/update/ppermute | solution.py:360
  296.8 19.3 %all-to-all-start.7 = ((f32[64,1,3]{2,1,0:T(1,128)}), f32[64,1,3]{2,1,0:T(1,128)S(1)}, u32[]{:S(2)}, u32[]{:S(2)}) async-start(f32[64,1,3]{2,1,0:T(1,128)} %broadcast_in_dim.13), calls=%async_computation.7 | async-start | bytes 65536 | tf_op jit(solution)/shard_map/signal/all_to_all | solution.py:475
  310.2 6.8 %copy-start.1 = (bf16[3,1024,256]{2,1,0:T(8,128)(2,1)S(1)}, bf16[3,1024,256]{2,1,0:T(8,128)(2,1)}, u32[]{:S(2)}) copy-start(bf16[3,1024,256]{2,1,0:T(8,128)(2,1)} %param.13) | copy-start | bytes 4718596
Sparse Core Ops, SparseCore 0:
  12.3 79.6 all-gather.4
  184.3 77.5 all-gather.6

commit v3 on v2

--- a/solution.py
+++ b/solution.py
@@ -153,13 +153,11 @@
 
 
 def middle_kernel(
-    where_ref, square0_ref, square1_ref, square2_ref, square3_ref, own_ref, row1_ref, row2_ref,
-    row3_ref, col1_ref, col2_ref, col3_ref, columns_ref, precoded_ref, slots_ref, gram_ref,
+    where_ref, square_ref, own_ref, row1_ref, row2_ref, row3_ref, col1_ref, col2_ref, col3_ref, columns_ref, precoded_ref, slots_ref, gram_ref,
     place_ref, first_out, block1_out, block2_out, block3_out, packed_out,
 ):
     y, row, first = where_ref[0], where_ref[1], where_ref[2]
     user_rows = own_ref.shape[0]
-    squares = [square0_ref, square1_ref, square2_ref, square3_ref]
     by_row = [own_ref, row1_ref, row2_ref, row3_ref]
     by_col = [own_ref, col1_ref, col2_ref, col3_ref]
     outs = [first_out, block1_out, block2_out, block3_out]
@@ -167,9 +165,9 @@
     choose = (ids == place_ref[...]).astype(f32).astype(bf16)
     schur = -t_dot(choose, gram_ref[...].astype(bf16))
     for d in range(4):
-        block = dot(squares[d][y], own_ref[...])
+        block = dot(square_ref[y, d], own_ref[...])
         for e in range(1, 4):
-            block += dot(squares[d][(y + e) % 4], by_col[e][...])
+            block += dot(square_ref[(y + e) % 4, d], by_col[e][...])
         low = block.astype(bf16)
         outs[d][...] = block if d == 0 else low
         schur += t_dot(by_row[d][...], low)
@@ -178,7 +176,7 @@
     packed_out[:, TOTAL:] = split(t_dot, border, precoded_ref[...]).astype(bf16)
 
 
-def make_middle(where, squares, by_row, by_col, columns, precoded, slot_plane, gram, place_plane):
+def make_middle(where, square, by_row, by_col, columns, precoded, slot_plane, gram, place_plane):
     shape = columns.shape
     return pl.pallas_call(
         middle_kernel,
@@ -189,12 +187,12 @@
             jax.ShapeDtypeStruct(shape, bf16),
             jax.ShapeDtypeStruct((TOTAL, TOTAL + STREAMS), bf16),
         ),
-        in_specs=[SMEM] + [VMEM] * 16,
+        in_specs=[SMEM] + [VMEM] * 13,
         out_specs=(VMEM,) * 5,
         compiler_params=params(),
         cost_estimate=cost(2_000_000_000, 8_000_000),
         name="middle",
-    )(where, *squares, *by_row, *by_col[1:], columns, precoded, slot_plane, gram, place_plane)
+    )(where, square, *by_row, *by_col[1:], columns, precoded, slot_plane, gram, place_plane)
 
 
 def invert_block(a):
@@ -382,7 +380,12 @@
 
     with jax.named_scope("planes"):
         low = inverse.astype(bf16).reshape(group_count, user_rows, 4, user_rows)
-        full_rows = to_planes(low.transpose(0, 2, 1, 3))
+        low = low.transpose(2, 0, 1, 3)
+        pieces = []
+        for d in range(4):
+            piece = lax.dynamic_index_in_dim(low, (x_index + d) % 4, 0, keepdims=False)
+            pieces.append(along_x(piece, d) if d else piece)
+        square = to_planes(jnp.stack(pieces, axis=1))
         symbol_part = jnp.einsum(
             "grc,gcs->grs", inverse, symbols.astype(f32), precision=highest
         )
@@ -415,15 +418,9 @@
         ).reshape(1, TOTAL)
 
     with jax.named_scope("columns"):
-        squares = []
-        for d in range(4):
-            piece = lax.dynamic_index_in_dim(full_rows, (x_index + d) % 4, 1, keepdims=False)
-            squares.append(along_x(piece, d) if d in (1, 3) else piece)
-        gathered, squares, precoded = lax.optimization_barrier((gathered, squares, precoded))
-        squares[2] = along_x(squares[2], 2)
+        gathered, square, precoded = lax.optimization_barrier((gathered, square, precoded))
         both = make_columns(row_index.reshape(1), gathered, channels, place)
         both = lax.all_to_all(both, "col", 0, 0, tiled=True)
-        both, squares = lax.optimization_barrier((both, squares))
         summed = jnp.sum(both.astype(f32), axis=0)
         columns = summed[:user_rows]
         gram = summed[user_rows:]
@@ -434,8 +431,12 @@
     with jax.named_scope("schur"):
         where = jnp.stack([y_index, row_index, first_row])
         block0, block1, block2, block3, packed = make_middle(
-            where, squares, by_row, by_col, columns, precoded, slot_plane, gram, plane_place
+            where, square, by_row, by_col, columns, precoded, slot_plane, gram, plane_place
         )
+        weighted = block0
+        for d, block in ((1, block1), (2, block2), (3, block3)):
+            weighted = weighted + along_x(block, -d).astype(f32)
+        weighted_all = lax.all_gather(weighted.astype(bf16), "row")
         packed = packed.reshape(16, SHARE, TOTAL + STREAMS)
         shared = lax.all_to_all(packed, "row", 0, 0, tiled=True)
         shared = jnp.sum(shared.astype(f32), axis=0)
@@ -447,15 +448,10 @@
         ready = jnp.concatenate([schur_rows, shared[:, TOTAL:]], axis=1)
         ready = jnp.broadcast_to(ready[None], (16, SHARE, TOTAL + STREAMS))
         whole = lax.all_to_all(ready, "row", 0, 0, tiled=True).reshape(TOTAL, TOTAL + STREAMS)
-        ready, block1, block2, block3 = lax.optimization_barrier((ready, block1, block2, block3))
-        weighted = block0
-        for d, block in ((1, block1), (2, block2), (3, block3)):
-            weighted = weighted + along_x(block, -d).astype(f32)
 
     with jax.named_scope("users"):
         channel = make_channel(first_arg, gathered, channels, place, slots_mine)
-        whole, channel, weighted = lax.optimization_barrier((whole, channel, weighted))
-        weighted_all = lax.all_gather(weighted.astype(bf16), "row")
+        whole, channel = lax.optimization_barrier((whole, channel))
         schur_inverse, users = make_solve(first_arg, whole, weighted, precoded, slot_plane)
         users_side = lax.all_to_all(users, "col", 0, 0, tiled=True)
 

time: 325 us -> 278 us (0.86)
  waiting for transfers between devices: 156 us -> 100 us
  blocking collectives: 11.7 us -> 28.8 us
  starting transfers between devices: 61.4 us -> 51 us
    all_gather x1, waiting for transfers between devices: 43.8 us -> 0.02 us  [local(): weighted_all = lax.all_gather(weighted.astype(bf16), 'row')]
    all_to_all x1, waiting for transfers between devices: 0.01 us -> 23.9 us  [local(): received = lax.all_to_all(signal_part, 'row', 0, 0, tiled=True)]
    ppermute x3, waiting for transfers between devices: 18.5 us -> 0.01 us  [along_z(): return lax.ppermute(value, 'col', [(z, (z + step) % 4) for z in range(4)])]
    all_to_all x0 -> x1, blocking collectives: none -> 18.3 us  [local(): both = lax.all_to_all(both, 'col', 0, 0, tiled=True)]
    ppermute x9, waiting for transfers between devices: 36 us -> 21.2 us  [along_x(): return lax.ppermute(value, 'row', pairs)]
    all_to_all x1, starting transfers between devices: 9.83 us -> 4.6 us  [local(): power = lax.all_to_all(power, ('row', 'col'), 0, 0, tiled=True)]
    all_to_all x2, waiting for transfers between devices: 29.9 us -> 25 us  [to_planes(): return lax.all_to_all(padded, 'col', 0, 0, tiled=True)]
    all_to_all x1 -> x0, starting transfers between devices: 4.44 us -> none  [local(): both = lax.all_to_all(both, 'col', 0, 0, tiled=True)]
  transfers between devices with their start and end apart: 25 -> 24, of which waited for: 18 -> 16; matrix products, arithmetic and copies ran while one was open for 8% -> 11% of each run, Pallas kernels for 8% -> 10%
where the time goes in v3:
time: 278 us; the launch traced here: 277 us
  waiting for transfers between devices  100 us (36%)
  starting transfers between devices  51 us (18%)
  Pallas kernels  40.8 us (15%)
  blocking collectives  28.8 us (10%)
  other arithmetic  20.8 us (7%)
  local copies, waits for them, and re-layouts  18.9 us (7%)
  between operations  14.6 us (5%)
    all_to_all x2, waiting for transfers between devices, to_planes(): return lax.all_to_all(padded, 'col', 0, 0, tiled=True)  25 us
    all_to_all x1, waiting for transfers between devices, local(): received = lax.all_to_all(signal_part, 'row', 0, 0, tiled=True)  23.9 us
    ppermute x9, waiting for transfers between devices, along_x(): return lax.ppermute(value, 'row', pairs)  21.2 us
    all_to_all x1, blocking collectives, local(): both = lax.all_to_all(both, 'col', 0, 0, tiled=True)  18.3 us
    pallas_call x1, Pallas kernels, make_solve(): pl.pallas_call(solve_kernel, out_shape=(jax.ShapeDtypeStruct((TOTAL, TOTA...  13.9 us
    ppermute x9, starting transfers between devices, along_x(): return lax.ppermute(value, 'row', pairs)  13.6 us
    all_to_all x1, waiting for transfers between devices, local(): shared = lax.all_to_all(packed, 'row', 0, 0, tiled=True)  11.1 us
    all_to_all x2, starting transfers between devices, to_planes(): return lax.all_to_all(padded, 'col', 0, 0, tiled=True)  10.5 us
  transfers between devices with their start and end apart: 24, of which 16 were waited for; matrix products, arithmetic and copies ran while one was open for 11% of the time, Pallas kernels for 10%

profile of v3, /device:TPU:0, one launch (start us, length us, event | category | flops | bytes accessed | tf_op | source)
XLA Modules:
  0.0 276.9 jit_solution(15624941234907011228)
XLA Ops:
  7.2 1.1 constant_dynamic-slice_fusion.7
  8.4 1.6 collective-permute-done
  10.0 1.0 select_bitcast_fusion.1
  11.3 0.9 pad.6
  12.3 3.3 %convert_element_type.47 = bf16[3,256,1024]{2,1,0:T(8,128)(2,1)} convert(f32[3,256,1024]{2,1,0:T(8,128)} %param.8) | non-fusion elementwise | flops 786432 | bytes 4718592 | tf_op jit(solution)/shard_map/planes/convert_element_type | solution.py:382
  15.6 2.9 %reshape.285 = bf16[3,256,4,256]{3,2,1,0:T(4,128)(2,1)S(1)} reshape(bf16[3,256,1024]{2,1,0:T(8,128)(2,1)} %convert_element_type.47) | data formatting | bytes 3145728 | tf_op jit(solution)/shard_map/planes/reshape | solution.py:382
  18.5 4.0 %constant_dynamic-slice_fusion.6 = (bf16[3,256,1,256]{3,2,1,0:T(2,128)(2,1)}, bf16[3,256,1,256]{3,2,1,0:T(2,128)(2,1)S(1)}, bf16[3,256,1,256]{3,2,1,0:T(2,128)(2,1)S(1)}, bf16[3,256,1,256]{3,2,1,0:T(2,128)(2,1)S(1)}) fusion(bf16[3,256,4,256]{3,2,1,0:T(4,128)(2,1)S(1)} %reshape.285, s32[]{:T(128)S(6)} %select_n.184, s32[]{:T(128)S(6)} %select_n.188, ...), kind=kLoop, calls=%fused_computation.60 | loop fusion | bytes 3145744 | tf_op jit(solution)/shard_map/dynamic-slice
  22.6 0.8 copy.51
  23.4 3.1 %collective-permute-start.2 = (bf16[3,256,256]{2,1,0:T(8,128)(2,1)}, bf16[3,256,256]{2,1,0:T(8,128)(2,1)S(1)}, u32[]{:S(2)}, u32[]{:S(2)}) collective-permute-start(bf16[3,256,256]{2,1,0:T(8,128)(2,1)} %bitcast.64), channel_id=1, source_target_pairs={{0,8},{4,12},{8,0},{12,4},{16,24},{20,28},{24,16},{28,20},{32,40},... | collective-permute-start | bytes 1179656 | tf_op jit(solution)/shard_map/planes/ppermute | solution.py:351
  26.5 0.8 copy.50
  27.3 1.1 collective-permute-start.3
  28.5 0.8 copy.52
  29.3 0.9 collective-permute-start.1
  30.2 1.6 fusion.22
  31.8 1.2 concatenate.10
  33.0 5.3 %all-to-all-start.1 = ((f32[4,256,256]{2,1,0:T(8,128)}), f32[4,256,256]{2,1,0:T(8,128)S(1)}, u32[]{:S(2)}, u32[]{:S(2)}) async-start(f32[4,256,256]{2,1,0:T(8,128)} %concatenate.10), calls=%async_computation.1 | async-start | bytes 2097152 | tf_op jit(solution)/shard_map/planes/all_to_all | solution.py:362
  38.4 4.0 %collective-permute-done.2 = bf16[3,256,256]{2,1,0:T(8,128)(2,1)S(1)} collective-permute-done((bf16[3,256,256]{2,1,0:T(8,128)(2,1)}, bf16[3,256,256]{2,1,0:T(8,128)(2,1)S(1)}, u32[]{:S(2)}, u32[]{:S(2)}) %collective-permute-start.2) | collective-permute-done | bytes 393248 | tf_op jit(solution)/shard_map/planes/ppermute | solution.py:351
  42.4 9.5 %collective-permute-done.3 = bf16[3,256,256]{2,1,0:T(8,128)(2,1)S(1)} collective-permute-done((bf16[3,256,256]{2,1,0:T(8,128)(2,1)}, bf16[3,256,256]{2,1,0:T(8,128)(2,1)S(1)}, u32[]{:S(2)}, u32[]{:S(2)}) %collective-permute-start.3) | collective-permute-done | bytes 393248 | tf_op jit(solution)/shard_map/planes/ppermute | solution.py:351
  52.2 2.4 fusion.6
  54.5 5.2 %all-to-all-start = ((bf16[4,4,256,256]{3,2,1,0:T(8,128)(2,1)}), bf16[4,4,256,256]{3,2,1,0:T(8,128)(2,1)S(1)}, u32[]{:S(2)}, u32[]{:S(2)}) async-start(bf16[4,4,256,256]{3,2,1,0:T(8,128)(2,1)} %fusion.6), calls=%async_computation | async-start | bytes 4194304 | tf_op jit(solution)/shard_map/planes/all_to_all | solution.py:362
  61.1 25.0 %all-to-all-done.square_ref = bf16[4,4,256,256]{3,2,1,0:T(8,128)(2,1)S(1)} async-done(((bf16[4,4,256,256]{3,2,1,0:T(8,128)(2,1)}), bf16[4,4,256,256]{3,2,1,0:T(8,128)(2,1)S(1)}, u32[]{:S(2)}, u32[]{:S(2)}) %all-to-all-start) | async-done | bytes 2097184 | tf_op jit(solution)/shard_map/planes/all_to_all | solution.py:362
  86.1 5.2 %all-gather.5.cloned.1.call-done = bf16[1792,2048]{1,0:T(8,128)(2,1)} async-done(((bf16[112,2048]{1,0:T(8,128)(2,1)}), bf16[1792,2048]{1,0:T(8,128)(2,1)}) %all-gather.5.cloned.1.call-update) | async-done | bytes 7340048 | tf_op jit(solution)/shard_map/newcomers/all_gather | solution.py:379
  91.3 9.7 %columns.1 = bf16[4,304,384]{2,1,0:T(8,128)(2,1)} custom-call(s32[1]{0:T(128)} %bitcast.3.row_ref, bf16[16,112,2048]{2,1,0:T(8,128)(2,1)} %bitcast.81, bf16[3,256,2048]{2,1,0:T(8,128)(2,1)} %channel_ref.3, s32[3,1,384]{2,1,0:T(1,128)} %fusion.17.place_ref), custom_call_target="tpu_custom_call" | custom-call | flops 4000000000 | bytes 12000000 | tf_op jit(solution)/shard_map/columns/columns/pallas_call | solution.py:115
  101.1 18.3 %all_to_all.40 = bf16[4,304,384]{2,1,0:T(8,128)(2,1)S(1)} all-to-all(bf16[4,304,384]{2,1,0:T(8,128)(2,1)} %columns.1), channel_id=1, replica_groups=mesh['grp'=2,'row'=16,'col'=4] {'col'}, dimensions={0} | all-to-all | bytes 1867776 | tf_op jit(solution)/shard_map/columns/all_to_all | solution.py:423
  119.5 1.7 collective-permute-start.4
  121.3 2.7 collective-permute-start.5
  123.9 1.4 collective-permute-start.6
  125.4 1.2 collective-permute-start.7
  126.6 1.1 collective-permute-start.8
  127.7 0.7 collective-permute-done.4.row1_ref
  128.4 3.6 %collective-permute-start.9 = (bf16[256,384]{1,0:T(8,128)(2,1)S(1)}, bf16[256,384]{1,0:T(8,128)(2,1)S(1)}, u32[]{:S(2)}, u32[]{:S(2)}) collective-permute-start(bf16[256,384]{1,0:T(8,128)(2,1)S(1)} %slice.73.own_ref), channel_id=1, source_target_pairs={{0,16},{4,20},{8,24},{12,28},{16,32},{20,36},{24,40},{28,44},{32,4... | collective-permute-start | bytes 589832 | tf_op jit(solution)/shard_map/columns/ppermute | solution.py:355
  132.8 2.6 collective-permute-done.8.col2_ref
  135.4 2.0 collective-permute-done.9.col3_ref
  137.4 3.6 %middle.1 = (f32[256,384]{1,0:T(8,128)S(1)}, bf16[256,384]{1,0:T(8,128)(2,1)S(1)}, bf16[256,384]{1,0:T(8,128)(2,1)S(1)}, bf16[256,384]{1,0:T(8,128)(2,1)S(1)}, bf16[384,640]{1,0:T(8,128)(2,1)}) custom-call(s32[3]{0:T(128)S(1)} %pad_add_fusion.where_ref, bf16[4,4,256,256]{3,2,1,0:T(8,128)(2,1)S(1)} %all-to-all-done.square_ref, ...), custom_call_target="tpu_custom_call" | custom-call | flops 2000000000 | bytes 8000000 | tf_op jit(solution)/shard_map/schur/middle/pallas_call | solution.py:181
  141.1 1.5 collective-permute-start.11
  142.5 1.2 collective-permute-start.12
  143.7 3.0 %collective-permute-done.10 = bf16[256,384]{1,0:T(8,128)(2,1)S(1)} collective-permute-done((bf16[256,384]{1,0:T(8,128)(2,1)S(1)}, bf16[256,384]{1,0:T(8,128)(2,1)S(1)}, u32[]{:S(2)}, u32[]{:S(2)}) %collective-permute-start.10) | collective-permute-done | bytes 196640 | tf_op jit(solution)/shard_map/schur/ppermute | solution.py:351
  146.7 1.6 collective-permute-done.11
  148.3 2.0 collective-permute-done.12
  150.3 0.8 fusion.21
  151.1 4.2 %all-to-all-start.3 = ((bf16[16,24,640]{2,1,0:T(8,128)(2,1)}), bf16[16,24,640]{2,1,0:T(8,128)(2,1)S(1)}, u32[]{:S(2)}, u32[]{:S(2)}) async-start(bf16[16,24,640]{2,1,0:T(8,128)(2,1)} %bitcast.15), calls=%async_computation.3 | async-start | bytes 983040 | tf_op jit(solution)/shard_map/schur/all_to_all | solution.py:441
  155.4 11.1 %all-to-all-done.3 = bf16[16,24,640]{2,1,0:T(8,128)(2,1)S(1)} async-done(((bf16[16,24,640]{2,1,0:T(8,128)(2,1)}), bf16[16,24,640]{2,1,0:T(8,128)(2,1)S(1)}, u32[]{:S(2)}, u32[]{:S(2)}) %all-to-all-start.3) | async-done | bytes 491552 | tf_op jit(solution)/shard_map/schur/all_to_all | solution.py:441
  166.7 1.0 broadcast_in_dim.12
  167.7 3.9 %all-to-all-start.4 = ((f32[16,24,640]{2,1,0:T(8,128)}), f32[16,24,640]{2,1,0:T(8,128)S(1)}, u32[]{:S(2)}, u32[]{:S(2)}) async-start(f32[16,24,640]{2,1,0:T(8,128)} %broadcast_in_dim.12), calls=%async_computation.4 | async-start | bytes 1966080 | tf_op jit(solution)/shard_map/schur/all_to_all | solution.py:450
  172.2 8.2 %channel.1.channel_ref = bf16[3,256,2048]{2,1,0:T(8,128)(2,1)} custom-call(s32[1]{0:T(128)} %bitcast.1.first_ref, bf16[16,112,2048]{2,1,0:T(8,128)(2,1)} %bitcast.82, bf16[3,256,2048]{2,1,0:T(8,128)(2,1)} %channel_ref.3, s32[3,1,384]{2,1,0:T(1,128)} %fusion.17.place_ref, s32[3,1,384]{2,1,0:T(1,128)} %reshape.290.slots_ref), custom_call_target="tpu_custom_call" | custom-call | flops 4000000000 | bytes 14000000 | tf_op jit(solution)/shard_map/users/channel/pallas_call | solution.py:143
  180.4 3.8 %all-to-all-done.4 = f32[16,24,640]{2,1,0:T(8,128)S(1)} async-done(((f32[16,24,640]{2,1,0:T(8,128)}), f32[16,24,640]{2,1,0:T(8,128)S(1)}, u32[]{:S(2)}, u32[]{:S(2)}) %all-to-all-start.4) | async-done | bytes 983072 | tf_op jit(solution)/shard_map/schur/all_to_all | solution.py:450
  184.2 13.9 %solve.1 = (f32[384,384]{1,0:T(8,128)S(1)}, bf16[4,256,256]{2,1,0:T(8,128)(2,1)S(1)}) custom-call(s32[1]{0:T(128)} %bitcast.1.first_ref, f32[384,640]{1,0:T(8,128)S(1)} %bitcast.70, f32[256,384]{1,0:T(8,128)S(1)} %get-tuple-element.45.weighted_ref, f32[256,256]{1,0:T(8,128)S(1)} %reduce_sum.76.precoded_ref, s32[1,384]{1,0:T(1,128)S(1)} %bitcast.72), custom_call_target="tpu_custom_call" | custom-call | flops 10000000000 | bytes 4000000 | tf_op jit(solution)/shard_map/users/solve/pallas_call | solution.py:255
  198.2 10.5 %all_to_all.41.users_ref = bf16[4,256,256]{2,1,0:T(8,128)(2,1)S(1)} all-to-all(bf16[4,256,256]{2,1,0:T(8,128)(2,1)S(1)} %get-tuple-element.32), channel_id=1, replica_groups=mesh['grp'=2,'row'=16,'col'=4] {'col'}, dimensions={0} | all-to-all | bytes 1048576 | tf_op jit(solution)/shard_map/users/all_to_all | solution.py:456
  208.6 2.1 signal.1
  210.8 4.5 %all-to-all-start.6 = ((bf16[16,3,16,2048]{3,2,1,0:T(8,128)(2,1)}), bf16[16,3,16,2048]{3,2,1,0:T(8,128)(2,1)}, u32[]{:S(2)}, u32[]{:S(2)}) async-start(bf16[16,3,16,2048]{3,2,1,0:T(8,128)(2,1)} %signal.1), calls=%async_computation.6 | async-start | bytes 6291456 | tf_op jit(solution)/shard_map/signal/all_to_all | solution.py:466
  215.8 1.9 copy-done.3
  217.7 1.1 copy-done.5
  218.7 3.2 %update.1 = (bf16[256,1024]{1,0:T(8,128)(2,1)S(1)}, bf16[256,1024]{1,0:T(8,128)(2,1)S(1)}, bf16[256,1024]{1,0:T(8,128)(2,1)S(1)}, bf16[256,1024]{1,0:T(8,128)(2,1)S(1)}) custom-call(s32[2]{0:T(128)S(1)} %pad_add_fusion.1.where_ref, f32[256,384]{1,0:T(8,128)S(1)} %get-tuple-element.45.weighted_ref, f32[384,384]{1,0:T(8,128)S(1)} %copy-done.5, ...), custom_call_target="tpu_custom_call" | custom-call | flops 1500000000 | bytes 8000000 | tf_op jit(solution)/shard_map/update/update/pallas_call | solution.py:324
  222.0 0.6 collective-permute-start.13
  222.6 2.1 collective-permute-start.14
  224.7 0.8 collective-permute-start.15
  225.7 2.1 and_select_fusion
  227.8 23.9 %all-to-all-done.6 = bf16[16,3,16,2048]{3,2,1,0:T(8,128)(2,1)} async-done(((bf16[16,3,16,2048]{3,2,1,0:T(8,128)(2,1)}), bf16[16,3,16,2048]{3,2,1,0:T(8,128)(2,1)}, u32[]{:S(2)}, u32[]{:S(2)}) %all-to-all-start.6) | async-done | bytes 3145760 | tf_op jit(solution)/shard_map/signal/all_to_all | solution.py:466
  251.7 2.5 convert_reduce_fusion
  255.0 4.6 %all-to-all-start.7 = ((f32[64,1,3]{2,1,0:T(1,128)}), f32[64,1,3]{2,1,0:T(1,128)S(1)}, u32[]{:S(2)}, u32[]{:S(2)}) async-start(f32[64,1,3]{2,1,0:T(1,128)} %broadcast_in_dim.13), calls=%async_computation.7 | async-start | bytes 65536 | tf_op jit(solution)/shard_map/signal/all_to_all | solution.py:471
  259.6 3.6 %fusion.15 = (f32[1,256,1024]{2,1,0:T(8,128)S(1)}, f32[1,256,1024]{2,1,0:T(8,128)S(1)}, f32[1,256,1024]{2,1,0:T(8,128)S(1)}) fusion(f32[3,256,1024]{2,1,0:T(8,128)} %and_select_fusion, f32[3,256,1024]{2,1,0:T(8,128)} %param.8, bf16[256,1024]{1,0:T(8,128)(2,1)} %collective-permute-done.15, bf16[256,1024]{1,0:T(8,128)(2,1)} %collective-permute-done.14, ...), kind=kLoop, calls=%fused_computation.24 | loop fusion | flops 4718592 | bytes 11534345 | tf_op jit(solution)/shard_map/final/stack | solution.py:488
  263.3 1.9 pad_maximum_fusion
  265.1 4.0 %all-to-all-done.7 = f32[64,1,3]{2,1,0:T(1,128)S(1)} async-done(((f32[64,1,3]{2,1,0:T(1,128)}), f32[64,1,3]{2,1,0:T(1,128)S(1)}, u32[]{:S(2)}, u32[]{:S(2)}) %all-to-all-start.7) | async-done | bytes 800 | tf_op jit(solution)/shard_map/signal/all_to_all | solution.py:471
  269.2 0.8 multiply_bitcast_fusion
  (78 shorter events, 5.3 us)
Async XLA Ops:
  7.2 23.0 %copy-start = (bf16[3,1024,256]{2,1,0:T(8,128)(2,1)S(1)}, bf16[3,1024,256]{2,1,0:T(8,128)(2,1)}, u32[]{:S(2)}) copy-start(bf16[3,1024,256]{2,1,0:T(8,128)(2,1)} %param.13) | copy-start | bytes 4718596
  7.2 84.2 %all-gather.5.cloned.1.call-start = ((), (), s32[]{:S(2)}) async-start(), calls=%async_computation.8 | async-start | bytes 7798784 | tf_op jit(solution)/shard_map/newcomers/all_gather | solution.py:379
  8.3 1.7 collective-permute-start
  22.6 7.6 %copy-start.6 = (f32[3,256,1024]{2,1,0:T(8,128)S(1)}, f32[3,256,1024]{2,1,0:T(8,128)}, u32[]{:S(2)}) copy-start(f32[3,256,1024]{2,1,0:T(8,128)} %param.8) | copy-start | bytes 9437188
  23.4 19.0 %collective-permute-start.2 = (bf16[3,256,256]{2,1,0:T(8,128)(2,1)}, bf16[3,256,256]{2,1,0:T(8,128)(2,1)S(1)}, u32[]{:S(2)}, u32[]{:S(2)}) collective-permute-start(bf16[3,256,256]{2,1,0:T(8,128)(2,1)} %bitcast.64), channel_id=1, source_target_pairs={{0,8},{4,12},{8,0},{12,4},{16,24},{20,28},{24,16},{28,20},{32,40},... | collective-permute-start | bytes 1179656 | tf_op jit(solution)/shard_map/planes/ppermute | solution.py:351
  27.3 24.6 %collective-permute-start.3 = (bf16[3,256,256]{2,1,0:T(8,128)(2,1)}, bf16[3,256,256]{2,1,0:T(8,128)(2,1)S(1)}, u32[]{:S(2)}, u32[]{:S(2)}) collective-permute-start(bf16[3,256,256]{2,1,0:T(8,128)(2,1)} %bitcast.63), channel_id=1, source_target_pairs={{0,12},{4,0},{8,4},{12,8},{16,28},{20,16},{24,20},{28,24},{32,44},... | collective-permute-start | bytes 1179656 | tf_op jit(solution)/shard_map/planes/ppermute | solution.py:351
  29.3 22.9 %collective-permute-start.1 = (bf16[3,256,256]{2,1,0:T(8,128)(2,1)}, bf16[3,256,256]{2,1,0:T(8,128)(2,1)}, u32[]{:S(2)}, u32[]{:S(2)}) collective-permute-start(bf16[3,256,256]{2,1,0:T(8,128)(2,1)} %bitcast.65), channel_id=1, source_target_pairs={{0,4},{4,8},{8,12},{12,0},{16,20},{20,24},{24,28},{28,16},{32,36},... | collective-permute-start | bytes 1179656 | tf_op jit(solution)/shard_map/planes/ppermute | solution.py:351
  31.8 6.5 %copy-start.7 = (bf16[3,256,1,256]{3,2,1,0:T(2,128)(2,1)S(1)}, bf16[3,256,1,256]{3,2,1,0:T(2,128)(2,1)}, u32[]{:S(2)}) copy-start(bf16[3,256,1,256]{3,2,1,0:T(2,128)(2,1)} %get-tuple-element.49) | copy-start | bytes 1179652
  33.0 21.6 %all-to-all-start.1 = ((f32[4,256,256]{2,1,0:T(8,128)}), f32[4,256,256]{2,1,0:T(8,128)S(1)}, u32[]{:S(2)}, u32[]{:S(2)}) async-start(f32[4,256,256]{2,1,0:T(8,128)} %concatenate.10), calls=%async_computation.1 | async-start | bytes 2097152 | tf_op jit(solution)/shard_map/planes/all_to_all | solution.py:362
  52.2 7.6 %copy-start.9 = (s32[6,3,128,1]{2,3,1,0:T(1,128)S(1)}, s32[6,3,128,1]{2,3,1,0:T(1,128)}, u32[]{:S(2)}) copy-start(s32[6,3,128,1]{2,3,1,0:T(1,128)} %param.10) | copy-start | bytes 27652
  52.2 7.9 %copy-start.10 = (s32[32]{0:T(128)S(1)}, s32[32]{0:T(128)}, u32[]{:S(2)}) copy-start(s32[32]{0:T(128)} %param.11) | copy-start | bytes 388
  54.5 31.6 %all-to-all-start = ((bf16[4,4,256,256]{3,2,1,0:T(8,128)(2,1)}), bf16[4,4,256,256]{3,2,1,0:T(8,128)(2,1)S(1)}, u32[]{:S(2)}, u32[]{:S(2)}) async-start(bf16[4,4,256,256]{3,2,1,0:T(8,128)(2,1)} %fusion.6), calls=%async_computation | async-start | bytes 4194304 | tf_op jit(solution)/shard_map/planes/all_to_all | solution.py:362
  59.8 156.0 %all-gather.7.cloned.1.call-start = ((), (), s32[]{:S(2)}) async-start(), calls=%async_computation.9 | async-start | bytes 3342336 | tf_op jit(solution)/shard_map/schur/all_gather | solution.py:439
  101.1 20.2 %copy-start.8 = (s32[6,3,128]{2,1,0:T(4,128)S(1)}, s32[6,3,128]{2,1,0:T(4,128)}, u32[]{:S(2)}) copy-start(s32[6,3,128]{2,1,0:T(4,128)} %param.12) | copy-start | bytes 27652
  119.5 8.9 %collective-permute-start.4 = (bf16[256,384]{1,0:T(8,128)(2,1)S(1)}, bf16[256,384]{1,0:T(8,128)(2,1)S(1)}, u32[]{:S(2)}, u32[]{:S(2)}) collective-permute-start(bf16[256,384]{1,0:T(8,128)(2,1)S(1)} %slice.73.own_ref), channel_id=1, source_target_pairs={{0,4},{4,8},{8,12},{12,0},{16,20},{20,24},{24,28},{28,16},{32,36},... | collective-permute-start | bytes 589832 | tf_op jit(solution)/shard_map/columns/ppermute | solution.py:351
  121.3 11.5 %collective-permute-start.5 = (bf16[256,384]{1,0:T(8,128)(2,1)S(1)}, bf16[256,384]{1,0:T(8,128)(2,1)S(1)}, u32[]{:S(2)}, u32[]{:S(2)}) collective-permute-start(bf16[256,384]{1,0:T(8,128)(2,1)S(1)} %slice.73.own_ref), channel_id=1, source_target_pairs={{0,8},{4,12},{8,0},{12,4},{16,24},{20,28},{24,16},{28,20},{32,40},... | collective-permute-start | bytes 589832 | tf_op jit(solution)/shard_map/columns/ppermute | solution.py:351
  123.9 8.9 %collective-permute-start.6 = (bf16[256,384]{1,0:T(8,128)(2,1)S(1)}, bf16[256,384]{1,0:T(8,128)(2,1)S(1)}, u32[]{:S(2)}, u32[]{:S(2)}) collective-permute-start(bf16[256,384]{1,0:T(8,128)(2,1)S(1)} %slice.73.own_ref), channel_id=1, source_target_pairs={{0,12},{4,0},{8,4},{12,8},{16,28},{20,16},{24,20},{28,24},{32,44},... | collective-permute-start | bytes 589832 | tf_op jit(solution)/shard_map/columns/ppermute | solution.py:351
  125.4 7.5 %collective-permute-start.7 = (bf16[256,384]{1,0:T(8,128)(2,1)S(1)}, bf16[256,384]{1,0:T(8,128)(2,1)S(1)}, u32[]{:S(2)}, u32[]{:S(2)}) collective-permute-start(bf16[256,384]{1,0:T(8,128)(2,1)S(1)} %slice.73.own_ref), channel_id=1, source_target_pairs={{0,48},{4,52},{8,56},{12,60},{16,0},{20,4},{24,8},{28,12},{32,16},... | collective-permute-start | bytes 589832 | tf_op jit(solution)/shard_map/columns/ppermute | solution.py:355
  126.6 8.8 %collective-permute-start.8 = (bf16[256,384]{1,0:T(8,128)(2,1)S(1)}, bf16[256,384]{1,0:T(8,128)(2,1)S(1)}, u32[]{:S(2)}, u32[]{:S(2)}) collective-permute-start(bf16[256,384]{1,0:T(8,128)(2,1)S(1)} %slice.73.own_ref), channel_id=1, source_target_pairs={{0,32},{4,36},{8,40},{12,44},{16,48},{20,52},{24,56},{28,60},{32,0... | collective-permute-start | bytes 589832 | tf_op jit(solution)/shard_map/columns/ppermute | solution.py:355
  128.4 9.0 %collective-permute-start.9 = (bf16[256,384]{1,0:T(8,128)(2,1)S(1)}, bf16[256,384]{1,0:T(8,128)(2,1)S(1)}, u32[]{:S(2)}, u32[]{:S(2)}) collective-permute-start(bf16[256,384]{1,0:T(8,128)(2,1)S(1)} %slice.73.own_ref), channel_id=1, source_target_pairs={{0,16},{4,20},{8,24},{12,28},{16,32},{20,36},{24,40},{28,44},{32,4... | collective-permute-start | bytes 589832 | tf_op jit(solution)/shard_map/columns/ppermute | solution.py:355
  141.1 5.7 %collective-permute-start.10 = (bf16[256,384]{1,0:T(8,128)(2,1)S(1)}, bf16[256,384]{1,0:T(8,128)(2,1)S(1)}, u32[]{:S(2)}, u32[]{:S(2)}) collective-permute-start(bf16[256,384]{1,0:T(8,128)(2,1)S(1)} %get-tuple-element.29), channel_id=1, source_target_pairs={{0,12},{4,0},{8,4},{12,8},{16,28},{20,16},{24,20},{28,24},{32,44},... | collective-permute-start | bytes 589832 | tf_op jit(solution)/shard_map/schur/ppermute | solution.py:351
  141.1 7.3 %collective-permute-start.11 = (bf16[256,384]{1,0:T(8,128)(2,1)S(1)}, bf16[256,384]{1,0:T(8,128)(2,1)S(1)}, u32[]{:S(2)}, u32[]{:S(2)}) collective-permute-start(bf16[256,384]{1,0:T(8,128)(2,1)S(1)} %get-tuple-element.30), channel_id=1, source_target_pairs={{0,8},{4,12},{8,0},{12,4},{16,24},{20,28},{24,16},{28,20},{32,40},... | collective-permute-start | bytes 589832 | tf_op jit(solution)/shard_map/schur/ppermute | solution.py:351
  142.5 7.8 %collective-permute-start.12 = (bf16[256,384]{1,0:T(8,128)(2,1)S(1)}, bf16[256,384]{1,0:T(8,128)(2,1)S(1)}, u32[]{:S(2)}, u32[]{:S(2)}) collective-permute-start(bf16[256,384]{1,0:T(8,128)(2,1)S(1)} %get-tuple-element.31), channel_id=1, source_target_pairs={{0,4},{4,8},{8,12},{12,0},{16,20},{20,24},{24,28},{28,16},{32,36},... | collective-permute-start | bytes 589832 | tf_op jit(solution)/shard_map/schur/ppermute | solution.py:351
  151.1 15.4 %all-to-all-start.3 = ((bf16[16,24,640]{2,1,0:T(8,128)(2,1)}), bf16[16,24,640]{2,1,0:T(8,128)(2,1)S(1)}, u32[]{:S(2)}, u32[]{:S(2)}) async-start(bf16[16,24,640]{2,1,0:T(8,128)(2,1)} %bitcast.15), calls=%async_computation.3 | async-start | bytes 983040 | tf_op jit(solution)/shard_map/schur/all_to_all | solution.py:441
  167.7 16.5 %all-to-all-start.4 = ((f32[16,24,640]{2,1,0:T(8,128)}), f32[16,24,640]{2,1,0:T(8,128)S(1)}, u32[]{:S(2)}, u32[]{:S(2)}) async-start(f32[16,24,640]{2,1,0:T(8,128)} %broadcast_in_dim.12), calls=%async_computation.4 | async-start | bytes 1966080 | tf_op jit(solution)/shard_map/schur/all_to_all | solution.py:450
  184.2 24.4 %copy-start.2 = (bf16[3,256,2048]{2,1,0:T(8,128)(2,1)S(1)}, bf16[3,256,2048]{2,1,0:T(8,128)(2,1)}, u32[]{:S(2)}) copy-start(bf16[3,256,2048]{2,1,0:T(8,128)(2,1)} %channel.1.channel_ref) | copy-start | bytes 9437188
  198.1 12.7 %copy-start.4 = (f32[384,384]{1,0:T(8,128)}, f32[384,384]{1,0:T(8,128)S(1)}, u32[]{:S(2)}) copy-start(f32[384,384]{1,0:T(8,128)S(1)} %get-tuple-element.34.inv_ref) | copy-start | bytes 1769476
  210.8 40.9 %all-to-all-start.6 = ((bf16[16,3,16,2048]{3,2,1,0:T(8,128)(2,1)}), bf16[16,3,16,2048]{3,2,1,0:T(8,128)(2,1)}, u32[]{:S(2)}, u32[]{:S(2)}) async-start(bf16[16,3,16,2048]{3,2,1,0:T(8,128)(2,1)} %signal.1), calls=%async_computation.6 | async-start | bytes 6291456 | tf_op jit(solution)/shard_map/signal/all_to_all | solution.py:466
  215.8 1.9 copy-start.3
  217.7 1.1 copy-start.5
  222.0 29.7 %collective-permute-start.13 = (bf16[256,1024]{1,0:T(8,128)(2,1)S(1)}, bf16[256,1024]{1,0:T(8,128)(2,1)S(1)}, u32[]{:S(2)}, u32[]{:S(2)}) collective-permute-start(bf16[256,1024]{1,0:T(8,128)(2,1)S(1)} %get-tuple-element.36), channel_id=1, source_target_pairs={{0,1},{1,2},{2,3},{3,0},{4,5},{5,6},{6,7},{7,4},{8,9},{9,10},{10,1... | collective-permute-start | bytes 1572872 | tf_op jit(solution)/shard_map/update/ppermute | solution.py:358
  222.6 29.1 %collective-permute-start.14 = (bf16[256,1024]{1,0:T(8,128)(2,1)S(1)}, bf16[256,1024]{1,0:T(8,128)(2,1)}, u32[]{:S(2)}, u32[]{:S(2)}) collective-permute-start(bf16[256,1024]{1,0:T(8,128)(2,1)S(1)} %get-tuple-element.37), channel_id=1, source_target_pairs={{0,2},{1,3},{2,0},{3,1},{4,6},{5,7},{6,4},{7,5},{8,10},{9,11},{10,... | collective-permute-start | bytes 1572872 | tf_op jit(solution)/shard_map/update/ppermute | solution.py:358
  224.7 27.1 %collective-permute-start.15 = (bf16[256,1024]{1,0:T(8,128)(2,1)S(1)}, bf16[256,1024]{1,0:T(8,128)(2,1)}, u32[]{:S(2)}, u32[]{:S(2)}) collective-permute-start(bf16[256,1024]{1,0:T(8,128)(2,1)S(1)} %get-tuple-element.38), channel_id=1, source_target_pairs={{0,3},{1,0},{2,1},{3,2},{4,7},{5,4},{6,5},{7,6},{8,11},{9,8},{10,9... | collective-permute-start | bytes 1572872 | tf_op jit(solution)/shard_map/update/ppermute | solution.py:358
  255.0 14.1 %all-to-all-start.7 = ((f32[64,1,3]{2,1,0:T(1,128)}), f32[64,1,3]{2,1,0:T(1,128)S(1)}, u32[]{:S(2)}, u32[]{:S(2)}) async-start(f32[64,1,3]{2,1,0:T(1,128)} %broadcast_in_dim.13), calls=%async_computation.7 | async-start | bytes 65536 | tf_op jit(solution)/shard_map/signal/all_to_all | solution.py:471
  263.2 6.8 %copy-start.1 = (bf16[3,1024,256]{2,1,0:T(8,128)(2,1)S(1)}, bf16[3,1024,256]{2,1,0:T(8,128)(2,1)}, u32[]{:S(2)}) copy-start(bf16[3,1024,256]{2,1,0:T(8,128)(2,1)} %param.13) | copy-start | bytes 4718596
Sparse Core Ops, SparseCore 0:
  12.4 78.9 all-gather.4
  151.3 50.3 all-gather.6
